TPU v7x, 512 devices: a whole 4x4x16 slice. The times are simulated.
512 devices in a mesh: epoch: 16 (over x, y), tile: 32 (over z, core).
Axes of the slice: x: 4, y: 4, z: 16, core: 2. Of those that a mesh axis runs over, the one named last changes fastest.
Arguments:
- anomaly: bfloat16 [64, 3072, 2048], P('epoch', 'tile'), may hold values from -120 to 120
- mask: int32 [64, 3072, 2048], P('epoch', 'tile'), may hold values 0 or 1
- epoch_weight: float32 [64], replicated, may hold values from 0.25 to 4
- days: int32 [64], replicated, may hold values from 0 to 3652
- window: int32 [32, 16], P('tile', 'epoch'), may hold values from 1 to 16, as said below
Outputs:
- rate: float32 [3072, 2048], P('tile', 'epoch')
- curvature: float32 [3, 3072, 2048], P(None, 'tile', 'epoch')
Inputs may be any that keep to these rules, and one draw needn't show every extreme that they name: `window`: one half-width for each block of the region; some block has 16.
All inputs are finite; a program needn't handle non-finite values. No bound on the sum of `mask` on one device may be relied on, other than what follows from the above.
Results may differ from a plain program's by a relative error of at most 0.0027.
Values may be sent and summed in bfloat16 or wider, within the bound.
No kernel may reach another device: no remote copies, remote signals or barrier semaphores. Data moves between devices by JAX's collectives and lax.ppermute only.
A program may use at most 64 MiB of HBM per device.

v0:
```python
import jax
import jax.numpy as jnp
from jax import lax
from jax.sharding import PartitionSpec as P

MAXH = 16


def extended(cells, sides, width):
    for axis, dim in sides:
        count = lax.axis_size(axis)
        ends = count - 1
        head = lax.slice_in_dim(cells, 0, width, axis=dim)
        tail = lax.slice_in_dim(cells, cells.shape[dim] - width, cells.shape[dim], axis=dim)
        cells = jnp.concatenate(
            [
                lax.ppermute(tail, axis, [(i, (i + 1) % count) for i in range(ends)]),
                cells,
                lax.ppermute(head, axis, [((i + 1) % count, i) for i in range(ends)]),
            ],
            axis=dim,
        )
    return cells


def tap_values(offset, width):
    inside = (jnp.abs(offset) <= width).astype(jnp.float32)
    scaled = offset / width
    middle = (width + 1.0) / (3.0 * width)
    return (inside, inside * scaled, inside * (scaled * scaled - middle))


def window_norms(width):
    taps = jnp.arange(-MAXH, MAXH + 1).astype(jnp.float32)
    flat, slope, bowl = tap_values(taps, width)
    count = 2.0 * width + 1.0
    return (count, jnp.sum(slope * slope), jnp.sum(bowl * bowl))


def fit_taps(padded, half):
    width = half.astype(jnp.float32)
    rows = padded.shape[0] - 2 * MAXH
    cols = padded.shape[1] - 2 * MAXH
    count, slope_norm, bowl_norm = window_norms(width)

    def across_step(index, totals):
        offset = index - half
        piece = lax.dynamic_slice_in_dim(padded, MAXH + offset, cols, 1)
        flat, slope, bowl = tap_values(offset.astype(jnp.float32), width)
        return (totals[0] + flat * piece, totals[1] + slope * piece, totals[2] + bowl * piece)

    wide = jnp.zeros((rows + 2 * MAXH, cols), jnp.float32)
    row_flat, row_slope, row_bowl = lax.fori_loop(0, 2 * half + 1, across_step, (wide, wide, wide))

    def along_step(index, totals):
        offset = index - half
        flat, slope, bowl = tap_values(offset.astype(jnp.float32), width)
        return (
            totals[0] + flat * lax.dynamic_slice_in_dim(row_bowl, MAXH + offset, rows, 0),
            totals[1] + bowl * lax.dynamic_slice_in_dim(row_flat, MAXH + offset, rows, 0),
            totals[2] + slope * lax.dynamic_slice_in_dim(row_slope, MAXH + offset, rows, 0),
        )

    narrow = jnp.zeros((rows, cols), jnp.float32)
    bowl_x, bowl_y, twist = lax.fori_loop(0, 2 * half + 1, along_step, (narrow, narrow, narrow))
    return jnp.stack(
        [
            bowl_x * (2.0 / (count * bowl_norm)),
            bowl_y * (2.0 / (count * bowl_norm)),
            twist / (slope_norm * slope_norm),
        ]
    )


def normal_sums(level, weight, moments):
    heavy = weight.astype(jnp.float32)
    timed = moments[:, None, None]
    loaded = heavy * level.astype(jnp.float32)
    return (
        jnp.sum(heavy, 0),
        jnp.sum(heavy * timed, 0),
        jnp.sum(heavy * timed * timed, 0),
        jnp.sum(loaded, 0),
        jnp.sum(loaded * timed, 0),
    )


def slope_from(sums):
    lifted = sums[0] + 1.0
    return (lifted * sums[4] - sums[1] * sums[3]) / (lifted * (sums[2] + 1.0) - sums[1] * sums[1])


def per_device(anomaly, mask, epoch_weight, days, window):
    own_count = anomaly.shape[0]
    first = lax.axis_index("epoch") * own_count
    tau = (days.astype(jnp.float32) - 1826.5) / 365.25
    own_quality = lax.dynamic_slice_in_dim(epoch_weight, first, own_count)
    weight = (mask.astype(jnp.float32) * own_quality[:, None, None]).astype(jnp.bfloat16)
    rate = slope_from(
        normal_sums(
            lax.all_to_all(anomaly, "epoch", split_axis=2, concat_axis=0, tiled=True),
            lax.all_to_all(weight, "epoch", split_axis=2, concat_axis=0, tiled=True),
            tau,
        )
    )
    padded = extended(rate, (("epoch", 1), ("tile", 0)), MAXH)
    half = window[0, 0]
    curvature = fit_taps(padded, half)
    return (rate, curvature)


def solution(mesh):
    in_specs = (P("epoch", "tile", None), P("epoch", "tile", None), P(), P(), P("tile", "epoch"))
    out_specs = (P("tile", "epoch"), P(None, "tile", "epoch"))
    return jax.shard_map(
        per_device, mesh=mesh, in_specs=in_specs, out_specs=out_specs, check_vma=False
    )
```

profile of v0, /device:TPU:224, one launch (start us, length us, event | category | flops | bytes accessed | tf_op | source)
XLA Modules:
  0.0 158.2 jit_solution(16570696043177995500)
XLA Ops:
  0.6 0.7 dynamic_slice.27
  1.4 2.3 %multiply_convert_fusion = bf16[4,96,2048]{2,1,0:T(8,128)(2,1)S(1)} fusion(s32[4,96,2048]{2,1,0:T(8,128)} %param.10, f32[4]{0:T(128)S(1)} %dynamic_slice.27), kind=kLoop, calls=%fused_computation.17 | loop fusion | flops 2359296 | bytes 4718608 | tf_op jit(solution)/shard_map/convert_element_type | solution.py:98
  3.7 2.6 %copy.15 = bf16[4,96,2048]{1,0,2:T(4,128)(2,1)} copy(bf16[4,96,2048]{2,1,0:T(8,128)(2,1)S(1)} %multiply_convert_fusion) | data formatting | bytes 3145728 | tf_op jit(solution)/shard_map/convert_element_type | solution.py:98
  6.3 7.0 %all-to-all-start = ((bf16[4,96,2048]{1,0,2:T(4,128)(2,1)}), bf16[4,96,2048]{1,0,2:T(4,128)(2,1)S(1)}, u32[]{:S(2)}, u32[]{:S(2)}) async-start(bf16[4,96,2048]{1,0,2:T(4,128)(2,1)} %copy.15), calls=%async_computation | async-start | bytes 4194304 | tf_op jit(solution)/shard_map/all_to_all | solution.py:102
  13.3 4.2 %copy.16 = bf16[4,96,2048]{1,0,2:T(4,128)(2,1)} copy(bf16[4,96,2048]{2,1,0:T(8,128)(2,1)} %param.9) | data formatting | bytes 3145728 | tf_op args[0]
  17.5 26.2 %all-to-all-done = bf16[4,96,2048]{1,0,2:T(4,128)(2,1)S(1)} async-done(((bf16[4,96,2048]{1,0,2:T(4,128)(2,1)}), bf16[4,96,2048]{1,0,2:T(4,128)(2,1)S(1)}, u32[]{:S(2)}, u32[]{:S(2)}) %all-to-all-start) | async-done | bytes 1572896 | tf_op jit(solution)/shard_map/all_to_all | solution.py:102
  43.7 4.4 %all-to-all-start.1 = ((bf16[4,96,2048]{1,0,2:T(4,128)(2,1)}), bf16[4,96,2048]{1,0,2:T(4,128)(2,1)}, u32[]{:S(2)}, u32[]{:S(2)}) async-start(bf16[4,96,2048]{1,0,2:T(4,128)(2,1)} %copy.16), calls=%async_computation.1 | async-start | bytes 4194304 | tf_op jit(solution)/shard_map/all_to_all | solution.py:101
  48.2 27.6 %all-to-all-done.1 = bf16[4,96,2048]{1,0,2:T(4,128)(2,1)} async-done(((bf16[4,96,2048]{1,0,2:T(4,128)(2,1)}), bf16[4,96,2048]{1,0,2:T(4,128)(2,1)}, u32[]{:S(2)}, u32[]{:S(2)}) %all-to-all-start.1) | async-done | bytes 1572896 | tf_op jit(solution)/shard_map/all_to_all | solution.py:101
  75.8 8.0 %multiply_reduce_fusion = (f32[96,128]{0,1:T(8,128)S(1)}, f32[96,128]{0,1:T(8,128)S(1)}, f32[96,128]{0,1:T(8,128)S(1)}, f32[96,128]{0,1:T(8,128)S(1)}, f32[96,128]{0,1:T(8,128)S(1)}) fusion(bf16[4,96,16,128]{1,0,3,2:T(4,128)(2,1)} %bitcast.9, bf16[4,96,16,128]{1,0,3,2:T(4,128)(2,1)S(1)} %bitcast.39, f32[16,4]{1,0:T(8,128)S(1)} %mul.206), kind=kLoop, calls=%fused_computation.15 | loop fusion | flops 8589312 | bytes 3391744 | tf_op jit(solution)/shard_map/reduce_sum | solution.py:84
  83.9 2.5 %collective-permute-start = (f32[96,16]{0,1:T(8,128)S(1)}, f32[96,16]{0,1:T(8,128)S(1)}, u32[]{:S(2)}, u32[]{:S(2)}) collective-permute-start(f32[96,16]{0,1:T(8,128)S(1)} %get-tuple-element.334), channel_id=1, source_target_pairs={{0,32},{32,64},{64,96},{96,128},{128,160},{160,192},{192,224},{224... | collective-permute-start | bytes 18440 | tf_op jit(solution)/shard_map/ppermute | solution.py:17
  86.3 1.3 collective-permute-start.1
  87.7 4.2 %collective-permute-done.1 = f32[96,16]{0,1:T(8,128)S(1)} collective-permute-done((f32[96,16]{0,1:T(8,128)S(1)}, f32[96,16]{0,1:T(8,128)S(1)}, u32[]{:S(2)}, u32[]{:S(2)}) %collective-permute-start.1) | collective-permute-done | bytes 6176 | tf_op jit(solution)/shard_map/ppermute | solution.py:19
  92.0 1.9 %collective-permute-start.2 = (f32[16,160]{0,1:T(8,128)S(1)}, f32[16,160]{0,1:T(8,128)S(1)}, u32[]{:S(2)}, u32[]{:S(2)}) collective-permute-start(f32[16,160]{0,1:T(8,128)S(1)} %get-tuple-element.332), channel_id=1, source_target_pairs={{0,1},{1,2},{2,3},{3,4},{4,5},{5,6},{6,7},{7,8},{8,9},{9,10},{10,1... | collective-permute-start | bytes 30728 | tf_op jit(solution)/shard_map/ppermute | solution.py:17
  93.9 3.6 %collective-permute-start.3 = (f32[16,160]{0,1:T(8,128)S(1)}, f32[16,160]{0,1:T(8,128)S(1)}, u32[]{:S(2)}, u32[]{:S(2)}) collective-permute-start(f32[16,160]{0,1:T(8,128)S(1)} %get-tuple-element.333), channel_id=1, source_target_pairs={{1,0},{2,1},{3,2},{4,3},{5,4},{6,5},{7,6},{8,7},{9,8},{10,9},{11,1... | collective-permute-start | bytes 30728 | tf_op jit(solution)/shard_map/ppermute | solution.py:19
  98.3 0.6 fusion.9
  100.8 0.7 copy.18
  101.5 0.1 pad_maximum_fusion.2
  101.7 29.5 %while.32 = (s32[]{:T(128)}, f32[128,128]{1,0:T(8,128)S(1)}, f32[128,128]{1,0:T(8,128)S(1)}, f32[128,128]{1,0:T(8,128)S(1)}, s32[]{:T(128)}, /*index=5*/s32[]{:T...) while((s32[]{:T(128)}, f32[128,128]{1,0:T(8,128)S(1)}, ...), condition=%wide.region_6.0_spmd, body=%wide.region_5.0_spmd.sunk | while | flops 98320 | bytes 721195 | solution.py:53
  102.4 0.1 copy.21
  103.3 0.1 copy.21
  104.2 0.1 copy.21
  106.0 0.1 copy.21
  131.2 26.3 %while.33 = (s32[]{:T(128)}, f32[96,128]{1,0:T(8,128)S(1)}, f32[96,128]{1,0:T(8,128)S(1)}, f32[96,128]{1,0:T(8,128)S(1)}, s32[]{:T(128)}, /*index=5*/s32[]{:T(12...) while((s32[]{:T(128)}, f32[96,128]{1,0:T(8,128)S(1)}, ...), condition=%wide.region_8.0_spmd, body=%wide.region_7.0_spmd.sunk | while | flops 73744 | bytes 442687 | solution.py:65
  157.6 0.7 pad_maximum_fusion
  (181 shorter events, 6.3 us)
Async XLA Ops:
  6.3 37.4 %all-to-all-start = ((bf16[4,96,2048]{1,0,2:T(4,128)(2,1)}), bf16[4,96,2048]{1,0,2:T(4,128)(2,1)S(1)}, u32[]{:S(2)}, u32[]{:S(2)}) async-start(bf16[4,96,2048]{1,0,2:T(4,128)(2,1)} %copy.15), calls=%async_computation | async-start | bytes 4194304 | tf_op jit(solution)/shard_map/all_to_all | solution.py:102
  13.3 34.8 %copy-start = (s32[64]{0:T(128)S(1)}, s32[64]{0:T(128)}, u32[]{:S(2)}) copy-start(s32[64]{0:T(128)} %param.12) | copy-start | bytes 772
  43.7 32.1 %all-to-all-start.1 = ((bf16[4,96,2048]{1,0,2:T(4,128)(2,1)}), bf16[4,96,2048]{1,0,2:T(4,128)(2,1)}, u32[]{:S(2)}, u32[]{:S(2)}) async-start(bf16[4,96,2048]{1,0,2:T(4,128)(2,1)} %copy.16), calls=%async_computation.1 | async-start | bytes 4194304 | tf_op jit(solution)/shard_map/all_to_all | solution.py:101
  83.9 3.8 %collective-permute-start = (f32[96,16]{0,1:T(8,128)S(1)}, f32[96,16]{0,1:T(8,128)S(1)}, u32[]{:S(2)}, u32[]{:S(2)}) collective-permute-start(f32[96,16]{0,1:T(8,128)S(1)} %get-tuple-element.334), channel_id=1, source_target_pairs={{0,32},{32,64},{64,96},{96,128},{128,160},{160,192},{192,224},{224... | collective-permute-start | bytes 18440 | tf_op jit(solution)/shard_map/ppermute | solution.py:17
  86.3 5.5 %collective-permute-start.1 = (f32[96,16]{0,1:T(8,128)S(1)}, f32[96,16]{0,1:T(8,128)S(1)}, u32[]{:S(2)}, u32[]{:S(2)}) collective-permute-start(f32[96,16]{0,1:T(8,128)S(1)} %get-tuple-element.335), channel_id=1, source_target_pairs={{32,0},{64,32},{96,64},{128,96},{160,128},{192,160},{224,192},{256... | collective-permute-start | bytes 18440 | tf_op jit(solution)/shard_map/ppermute | solution.py:19
  92.0 9.6 %collective-permute-start.2 = (f32[16,160]{0,1:T(8,128)S(1)}, f32[16,160]{0,1:T(8,128)S(1)}, u32[]{:S(2)}, u32[]{:S(2)}) collective-permute-start(f32[16,160]{0,1:T(8,128)S(1)} %get-tuple-element.332), channel_id=1, source_target_pairs={{0,1},{1,2},{2,3},{3,4},{4,5},{5,6},{6,7},{7,8},{8,9},{9,10},{10,1... | collective-permute-start | bytes 30728 | tf_op jit(solution)/shard_map/ppermute | solution.py:17
  93.9 7.6 %collective-permute-start.3 = (f32[16,160]{0,1:T(8,128)S(1)}, f32[16,160]{0,1:T(8,128)S(1)}, u32[]{:S(2)}, u32[]{:S(2)}) collective-permute-start(f32[16,160]{0,1:T(8,128)S(1)} %get-tuple-element.333), channel_id=1, source_target_pairs={{1,0},{2,1},{3,2},{4,3},{5,4},{6,5},{7,6},{8,7},{9,8},{10,9},{11,1... | collective-permute-start | bytes 30728 | tf_op jit(solution)/shard_map/ppermute | solution.py:19
where the time goes:
time: 161 us; the launch traced here: 158 us
  waiting for transfers between devices  58 us (36%)
  loops' own time  49.4 us (31%)
  starting transfers between devices  20.8 us (13%)
  other arithmetic  14.8 us (9%)
  local copies, waits for them, and re-layouts  11.7 us (7%)
  between operations  3.46 us (2%)
    all_to_all x1, waiting for transfers between devices, per_device(): lax.all_to_all(anomaly, 'epoch', split_axis=2, concat_axis=0, tiled=True)  27.6 us
    all_to_all x1, waiting for transfers between devices, per_device(): lax.all_to_all(weight, 'epoch', split_axis=2, concat_axis=0, tiled=True)  26.2 us
    another operation x1, loops' own time, fit_taps(): lax.fori_loop(0, 2 * half + 1, across_step, (wide, wide, wide))  24.9 us
    another operation x1, loops' own time, fit_taps(): lax.fori_loop(0, 2 * half + 1, along_step, (narrow, narrow, narrow))  24.5 us
    reduce_sum x1, other arithmetic, normal_sums(): jnp.sum(loaded * timed, 0)  8 us
    all_to_all x1, starting transfers between devices, per_device(): lax.all_to_all(weight, 'epoch', split_axis=2, concat_axis=0, tiled=True)  7.03 us
    ppermute x2, starting transfers between devices, extended(): lax.ppermute(head, axis, [((i + 1) % count, i) for i in range(ends)])  4.93 us
    unnamed x4, local copies, waits for them, and re-layouts  4.89 us
  transfers between devices with their start and end apart: 6, of which 3 were waited for; matrix products, arithmetic and copies ran while one was open for 4% of the time, Pallas kernels for 0%

commit v1 on v0

v1 whole, which is shorter than its diff:
```python
import functools

import jax
import jax.numpy as jnp
from jax import lax
from jax.experimental import pallas as pl
from jax.experimental.pallas import tpu as pltpu
from jax.sharding import PartitionSpec as P

MAXH = 16
SIDE = 4
OWN = 4
ROWS = 96
COLS = 128
TILES = 32
AXES = ("epoch", "tile")
STEPS = (2, 1, -1)
ANY = pl.BlockSpec(memory_space=pl.ANY)
SMEM = pl.BlockSpec(memory_space=pltpu.SMEM)
VMEM = pl.BlockSpec(memory_space=pltpu.VMEM)
HBM = pl.BlockSpec(memory_space=pltpu.HBM)
LIMIT = pltpu.CompilerParams(vmem_limit_bytes=8 << 20)
STRIP = 16


def ring_pairs(step, first):
    pairs = []
    for x in range(SIDE):
        for y in range(SIDE):
            for tile in range(TILES):
                if (tile % 2 == 0) == first:
                    there = (x + step) % SIDE * SIDE + y
                else:
                    there = x * SIDE + (y + step) % SIDE
                pairs.append(((x * SIDE + y) * TILES + tile, there * TILES + tile))
    return pairs


def shift(values, step, first):
    return lax.ppermute(values, AXES, ring_pairs(step, first))


def place():
    spot = lax.axis_index("epoch")
    even = lax.axis_index("tile") % 2 == 0
    x, y = spot // SIDE, spot % SIDE
    return jnp.where(even, x, y), jnp.where(even, y, x), even


def block_of(even, first, second):
    return jnp.where(even, SIDE * first + second, SIDE * second + first)


def epoch_of(even, first, second):
    return block_of(even, first, second) * OWN


def columns(block):
    return pl.ds(pl.multiple_of(block * COLS, COLS), COLS)


def pack_kernel(step, quality, anomaly, mask, out, valid, sems):
    first, second, even = place()
    there = (first + step + SIDE) % SIDE
    copies = []
    for slot in range(SIDE):
        cols = columns(block_of(even, there, slot))
        copies.append(
            (
                pltpu.make_async_copy(anomaly.at[:, :, cols], out.at[slot, pl.ds(0, OWN)], sems.at[slot, 0]),
                pltpu.make_async_copy(mask.at[:, :, cols], valid.at[slot], sems.at[slot, 1]),
            )
        )
    for level, seen in copies:
        seen.start()
    for level, seen in copies:
        level.start()
    base = epoch_of(even, first, second)
    for slot in range(SIDE):
        copies[slot][1].wait()
        for own in range(OWN):
            out[slot, OWN + own] = (valid[slot, own].astype(jnp.float32) * quality[base + own]).astype(jnp.bfloat16)
    for level, seen in copies:
        level.wait()


def pack(step, quality, anomaly, mask):
    return pl.pallas_call(
        functools.partial(pack_kernel, step),
        out_shape=jax.ShapeDtypeStruct((SIDE, 2 * OWN, ROWS, COLS), jnp.bfloat16),
        in_specs=[SMEM, HBM, HBM] if step == STEPS[0] else [SMEM, ANY, ANY],
        out_specs=VMEM,
        scratch_shapes=[
            pltpu.VMEM((SIDE, OWN, ROWS, COLS), jnp.int32),
            pltpu.SemaphoreType.DMA((SIDE, 2)),
        ],
        compiler_params=LIMIT,
        cost_estimate=pl.CostEstimate(flops=1 << 20, bytes_accessed=3 << 20, transcendentals=0),
        name="pack",
    )(quality, anomaly, mask)


def added(totals, heavy, height, moment):
    timed = heavy * moment
    loaded = heavy * height
    terms = (heavy, timed, timed * moment, loaded, loaded * moment)
    return terms if totals is None else tuple(map(jnp.add, totals, terms))


def moments_of(tau, even, first, second):
    base = epoch_of(even, first, second)
    return [tau[base + own] for own in range(OWN)]


def early_kernel(quality, tau, anomaly, mask, got, out, level, valid, sems):
    first, second, even = place()
    copies = []
    for slot in range(SIDE):
        cols = columns(block_of(even, first, slot))
        copies.append(pltpu.make_async_copy(anomaly.at[:, :, cols], level.at[slot], sems.at[slot, 0]))
        copies.append(pltpu.make_async_copy(mask.at[:, :, cols], valid.at[slot], sems.at[slot, 1]))
    for copy in copies:
        copy.start()
    for copy in copies:
        copy.wait()
    base = epoch_of(even, first, second)
    own_quality = [quality[base + own] for own in range(OWN)]
    own_moments = moments_of(tau, even, first, second)
    got_moments = moments_of(tau, even, (first - STEPS[0] + SIDE) % SIDE, second)
    for slot in range(SIDE):

        def rows(index, carry):
            at = pl.ds(pl.multiple_of(index * STRIP, STRIP), STRIP)
            totals = None
            for own in range(OWN):
                heavy = (valid[slot, own, at].astype(jnp.float32) * own_quality[own]).astype(jnp.bfloat16)
                height = level[slot, own, at].astype(jnp.float32)
                totals = added(totals, heavy.astype(jnp.float32), height, own_moments[own])
            for own in range(OWN):
                heavy = got[slot, OWN + own, at].astype(jnp.float32)
                height = got[slot, own, at].astype(jnp.float32)
                totals = added(totals, heavy, height, got_moments[own])
            for which, total in enumerate(totals):
                out[slot, which, at] = total
            return carry

        lax.fori_loop(0, ROWS // STRIP, rows, 0)


def early_sums(quality, tau, anomaly, mask, got):
    return pl.pallas_call(
        early_kernel,
        out_shape=jax.ShapeDtypeStruct((SIDE, 5, ROWS, COLS), jnp.float32),
        in_specs=[SMEM, SMEM, ANY, ANY, VMEM],
        out_specs=VMEM,
        scratch_shapes=[
            pltpu.VMEM((SIDE, OWN, ROWS, COLS), jnp.bfloat16),
            pltpu.VMEM((SIDE, OWN, ROWS, COLS), jnp.int32),
            pltpu.SemaphoreType.DMA((SIDE, 2)),
        ],
        compiler_params=LIMIT,
        cost_estimate=pl.CostEstimate(flops=1 << 23, bytes_accessed=3 << 20, transcendentals=0),
        name="early",
    )(quality, tau, anomaly, mask, got)


def late_kernel(step, tau, early, got_b, got_c, out):
    first, second, even = place()
    slot = (second + step + SIDE) % SIDE
    moments = [moments_of(tau, even, (first - moved + SIDE) % SIDE, second) for moved in STEPS[1:]]

    def rows(index, carry):
        at = pl.ds(pl.multiple_of(index * STRIP, STRIP), STRIP)
        totals = tuple(early[slot, which, at] for which in range(5))
        for got, moment in zip((got_b, got_c), moments):
            for own in range(OWN):
                heavy = got[slot, OWN + own, at].astype(jnp.float32)
                height = got[slot, own, at].astype(jnp.float32)
                totals = added(totals, heavy, height, moment[own])
        for which, total in enumerate(totals):
            out[which, at] = total
        return carry

    lax.fori_loop(0, ROWS // STRIP, rows, 0)


def late_sums(step, tau, early, got_b, got_c):
    return pl.pallas_call(
        functools.partial(late_kernel, step),
        out_shape=jax.ShapeDtypeStruct((5, ROWS, COLS), jnp.float32),
        in_specs=[SMEM, VMEM, VMEM, VMEM],
        out_specs=VMEM,
        compiler_params=LIMIT,
        cost_estimate=pl.CostEstimate(flops=1 << 21, bytes_accessed=1 << 20, transcendentals=0),
        name="late",
    )(tau, early, got_b, got_c)


GROUPS = ROWS // MAXH


def lane(shape):
    return lax.broadcasted_iota(jnp.int32, shape, 1)


def rate_kernel(own, got_a, got_b, got_c, rate, head, tail):
    total = [own[i] + got_a[i] + got_b[i] + got_c[i] for i in range(5)]
    lifted = total[0] + 1.0
    value = (lifted * total[4] - total[1] * total[3]) / (lifted * (total[2] + 1.0) - total[1] * total[1])
    rate[...] = value
    place_of = lane((MAXH, COLS)) // MAXH
    left = jnp.zeros((MAXH, COLS), jnp.float32)
    right = jnp.zeros((MAXH, COLS), jnp.float32)
    for group in range(GROUPS):
        piece = value[group * MAXH : (group + 1) * MAXH]
        here = place_of == group
        left = jnp.where(here, pltpu.roll(piece, group * MAXH, 1) if group else piece, left)
        right = jnp.where(here, pltpu.roll(piece, (group + 1) * MAXH, 1), right)
    head[...] = left
    tail[...] = right


def fitted_rate(own, got):
    strip = jax.ShapeDtypeStruct((MAXH, COLS), jnp.float32)
    return pl.pallas_call(
        rate_kernel,
        out_shape=(jax.ShapeDtypeStruct((ROWS, COLS), jnp.float32), strip, strip),
        in_specs=[VMEM] * 4,
        out_specs=(VMEM, VMEM, VMEM),
        compiler_params=LIMIT,
        name="rate",
    )(own, *got)


def sides_kernel(rate, before, after, sides, top, bottom):
    place_of = lane((MAXH, COLS)) // MAXH
    for group in range(GROUPS):
        back = (COLS - group * MAXH) % COLS
        left = pltpu.roll(before[...], back, 1) if back else before[...]
        right = pltpu.roll(after[...], (back + MAXH) % COLS, 1)
        piece = jnp.where(place_of == 0, left, jnp.where(place_of == 1, right, 0.0))
        sides[pl.ds(group * MAXH, MAXH)] = piece
        if group == 0:
            top[pl.ds(MAXH, MAXH)] = piece
        if group == GROUPS - 1:
            bottom[pl.ds(MAXH, MAXH)] = piece
    top[pl.ds(0, MAXH)] = rate[pl.ds(0, MAXH)]
    bottom[pl.ds(0, MAXH)] = rate[pl.ds(ROWS - MAXH, MAXH)]


def with_sides(rate, before, after):
    edge = jax.ShapeDtypeStruct((2 * MAXH, COLS), jnp.float32)
    return pl.pallas_call(
        sides_kernel,
        out_shape=(jax.ShapeDtypeStruct((ROWS, COLS), jnp.float32), edge, edge),
        in_specs=[VMEM] * 3,
        out_specs=(VMEM, VMEM, VMEM),
        compiler_params=LIMIT,
        name="sides",
    )(rate, before, after)


def three_parts(values):
    high = values.astype(jnp.bfloat16)
    rest = values - high.astype(jnp.float32)
    middle = rest.astype(jnp.bfloat16)
    low = (rest - middle.astype(jnp.float32)).astype(jnp.bfloat16)
    return high, middle, low


def taps(offset, half):
    inside = jnp.abs(offset) <= half
    flat = jnp.where(inside, 1.0, 0.0)
    slope = jnp.where(inside, offset, 0).astype(jnp.float32)
    return tuple(v.astype(jnp.bfloat16) for v in (flat, slope, slope * slope))


def product(left, right):
    return jnp.dot(left, right, preferred_element_type=jnp.float32)


def curve_kernel(window, rate, sides, above, below, out):
    half = window[0, 0]
    middle = (half * (half + 1)).astype(jnp.float32) / 3.0
    line = lax.broadcasted_iota(jnp.int32, (2 * COLS, COLS), 0)
    column = jnp.where(
        line < COLS, line,
        jnp.where(line < COLS + MAXH, line - COLS - MAXH, jnp.where(line < COLS + 2 * MAXH, line - MAXH, 4 * COLS)),
    )
    across = jnp.concatenate(taps(column - lane((2 * COLS, COLS)), half), axis=1)
    tall = ROWS + 2 * MAXH
    spot = lane((ROWS, tall))
    row = jnp.where(spot < ROWS, spot, jnp.where(spot < ROWS + MAXH, spot - ROWS - MAXH, spot - MAXH))
    along = taps(row - lax.broadcasted_iota(jnp.int32, (ROWS, tall), 0), half)

    main = jnp.concatenate([rate[...], above[pl.ds(0, MAXH)], below[pl.ds(0, MAXH)]], axis=0)
    beside = jnp.concatenate([sides[...], above[pl.ds(MAXH, MAXH)], below[pl.ds(MAXH, MAXH)]], axis=0)
    parts = three_parts(jnp.concatenate([main, beside], axis=1))
    wide = product(parts[0], across) + product(parts[1], across) + product(parts[2], across)
    flat, slope, square = (wide[:, i * COLS : (i + 1) * COLS] for i in range(3))
    bowl = square - middle * flat

    def down(weights, values):
        a, b, c = (product(weights, part) for part in three_parts(values))
        return a + b + c

    bowl_x = down(along[0], bowl)
    bowl_y = down(along[2], flat) - middle * down(along[0], flat)
    twist = down(along[1], slope)

    taps_at = lax.broadcasted_iota(jnp.int32, (8, COLS), 1) - MAXH
    inside = jnp.abs(taps_at) <= half
    squares = (taps_at * taps_at).astype(jnp.float32)
    width = half.astype(jnp.float32)
    slope_norm = jnp.sum(jnp.where(inside, squares, 0.0), axis=1, keepdims=True)[0:1]
    bowls = squares - middle
    bowl_norm = jnp.sum(jnp.where(inside, bowls * bowls, 0.0), axis=1, keepdims=True)[0:1]
    bowl_scale = 2.0 * width * width / ((2.0 * width + 1.0) * bowl_norm)
    twist_scale = width * width / (slope_norm * slope_norm)
    out[0] = bowl_x * bowl_scale
    out[1] = bowl_y * bowl_scale
    out[2] = twist * twist_scale


def curvature_of(window, rate, sides, above, below):
    return pl.pallas_call(
        curve_kernel,
        out_shape=jax.ShapeDtypeStruct((3, ROWS, COLS), jnp.float32),
        in_specs=[SMEM, VMEM, VMEM, VMEM, VMEM],
        out_specs=VMEM,
        compiler_params=LIMIT,
        name="curve",
    )(window, rate, sides, above, below)


def neighbour(values, axis, count, step):
    return lax.ppermute(values, axis, [(i, i + step) for i in range(count) if 0 <= i + step < count])


def per_device(anomaly, mask, epoch_weight, days, window):
    tau = (days.astype(jnp.float32) - 1826.5) / 365.25
    got = [shift(pack(step, epoch_weight, anomaly, mask), step, True) for step in STEPS]
    early = early_sums(epoch_weight, tau, anomaly, mask, got[0])
    mine = [late_sums(step, tau, early, got[1], got[2]) for step in STEPS + (0,)]
    rest = [shift(total, step, False) for step, total in zip(STEPS, mine)]
    rate, head, tail = fitted_rate(mine[3], rest)
    before = neighbour(tail, "epoch", SIDE * SIDE, 1)
    after = neighbour(head, "epoch", SIDE * SIDE, -1)
    sides, top, bottom = with_sides(rate, before, after)
    above = neighbour(bottom, "tile", TILES, 1)
    below = neighbour(top, "tile", TILES, -1)
    return rate, curvature_of(window, rate, sides, above, below)


def solution(mesh):
    in_specs = (P("epoch", "tile", None), P("epoch", "tile", None), P(), P(), P("tile", "epoch"))
    out_specs = (P("tile", "epoch"), P(None, "tile", "epoch"))
    return jax.shard_map(
        per_device, mesh=mesh, in_specs=in_specs, out_specs=out_specs, check_vma=False
    )
```

time: 161 us -> 74.5 us (0.46)
  the two profiles are of different devices: /device:TPU:224 before, /device:TPU:125 now
where the time goes in v1:
time: 74.5 us; the launch traced here: 74 us
  starting transfers between devices  34.5 us (46%)
  waiting for transfers between devices  22.9 us (31%)
  Pallas kernels  9.44 us (13%)
  local copies, waits for them, and re-layouts  5.57 us (7%)
  between operations  1.52 us (2%)
    ppermute x4, starting transfers between devices, neighbour(): lax.ppermute(values, axis, [(i, i + step) for i in range(count) if 0 <= i...  17.5 us
    ppermute x6, starting transfers between devices, shift(): return lax.ppermute(values, AXES, ring_pairs(step, first))  17 us
    ppermute x6, waiting for transfers between devices, shift(): return lax.ppermute(values, AXES, ring_pairs(step, first))  14.6 us
    ppermute x4, waiting for transfers between devices, neighbour(): lax.ppermute(values, axis, [(i, i + step) for i in range(count) if 0 <= i...  8.25 us
    unnamed x18, local copies, waits for them, and re-layouts  5.57 us
    pallas_call x4, Pallas kernels, late_sums(): pl.pallas_call(functools.partial(late_kernel, step), out_shape=jax.ShapeD...  3.06 us
    pallas_call x3, Pallas kernels, pack(): pl.pallas_call(functools.partial(pack_kernel, step), out_shape=jax.ShapeD...  2.86 us
    pallas_call x1, Pallas kernels, early_sums(): pl.pallas_call(early_kernel, out_shape=jax.ShapeDtypeStruct((SIDE, 5, ROW...  1.57 us
  transfers between devices with their start and end apart: 10, of which 7 were waited for; matrix products, arithmetic and copies ran while one was open for 0% of the time, Pallas kernels for 8%

profile of v1, /device:TPU:125, one launch (start us, length us, event | category | flops | bytes accessed | tf_op | source)
XLA Modules:
  0.0 74.0 jit_solution(3923342306413409229)
XLA Ops:
  0.6 1.9 %copy-done = s32[4,96,2048]{2,1,0:T(8,128)S(1)} copy-done((s32[4,96,2048]{2,1,0:T(8,128)S(1)}, s32[4,96,2048]{2,1,0:T(8,128)}, u32[]{:S(2)}) %copy-start) | copy-done | bytes 3145752
  2.5 1.4 %copy-done.2 = bf16[4,96,2048]{2,1,0:T(8,128)(2,1)S(1)} copy-done((bf16[4,96,2048]{2,1,0:T(8,128)(2,1)S(1)}, bf16[4,96,2048]{2,1,0:T(8,128)(2,1)}, u32[]{:S(2)}) %copy-start.2) | copy-done | bytes 1572888
  4.6 0.9 %pack.3 = bf16[4,8,96,128]{3,2,1,0:T(8,128)(2,1)S(1)} custom-call(f32[64]{0:T(128)S(1)} %copy-done.6, bf16[4,96,2048]{2,1,0:T(8,128)(2,1)S(1)} %copy-done.2, s32[4,96,2048]{2,1,0:T(8,128)S(1)} %copy-done), custom_call_target="tpu_custom_call" | custom-call | flops 1048576 | bytes 3145728 | tf_op jit(solution)/shard_map/pack/pallas_call | solution.py:88
  5.5 2.9 %collective-permute-start = (bf16[4,8,96,128]{3,2,1,0:T(8,128)(2,1)S(1)}, bf16[4,8,96,128]{3,2,1,0:T(8,128)(2,1)S(1)}, u32[]{:S(2)}, u32[]{:S(2)}) collective-permute-start(bf16[4,8,96,128]{3,2,1,0:T(8,128)(2,1)S(1)} %pack.3), channel_id=1, source_target_pairs={{0,256},{1,65},{2,258},{3,67},{4,260},{5,69},{6,262},{7,71},{8,264... | collective-permute-start | bytes 2359304 | tf_op jit(solution)/shard_map/ppermute | solution.py:40
  8.4 1.0 %pack.4 = bf16[4,8,96,128]{3,2,1,0:T(8,128)(2,1)S(1)} custom-call(f32[64]{0:T(128)S(1)} %copy-done.6, bf16[4,96,2048]{2,1,0:T(8,128)(2,1)S(1)} %copy-done.2, s32[4,96,2048]{2,1,0:T(8,128)S(1)} %copy-done), custom_call_target="tpu_custom_call" | custom-call | flops 1048576 | bytes 3145728 | tf_op jit(solution)/shard_map/pack/pallas_call | solution.py:88
  9.4 4.1 %collective-permute-start.1 = (bf16[4,8,96,128]{3,2,1,0:T(8,128)(2,1)S(1)}, bf16[4,8,96,128]{3,2,1,0:T(8,128)(2,1)S(1)}, u32[]{:S(2)}, u32[]{:S(2)}) collective-permute-start(bf16[4,8,96,128]{3,2,1,0:T(8,128)(2,1)S(1)} %pack.4), channel_id=1, source_target_pairs={{0,128},{1,33},{2,130},{3,35},{4,132},{5,37},{6,134},{7,39},{8,136... | collective-permute-start | bytes 2359304 | tf_op jit(solution)/shard_map/ppermute | solution.py:40
  13.5 1.0 %pack.5 = bf16[4,8,96,128]{3,2,1,0:T(8,128)(2,1)S(1)} custom-call(f32[64]{0:T(128)S(1)} %copy-done.6, bf16[4,96,2048]{2,1,0:T(8,128)(2,1)S(1)} %copy-done.2, s32[4,96,2048]{2,1,0:T(8,128)S(1)} %copy-done), custom_call_target="tpu_custom_call" | custom-call | flops 1048576 | bytes 3145728 | tf_op jit(solution)/shard_map/pack/pallas_call | solution.py:88
  14.5 1.9 %collective-permute-start.2 = (bf16[4,8,96,128]{3,2,1,0:T(8,128)(2,1)S(1)}, bf16[4,8,96,128]{3,2,1,0:T(8,128)(2,1)S(1)}, u32[]{:S(2)}, u32[]{:S(2)}) collective-permute-start(bf16[4,8,96,128]{3,2,1,0:T(8,128)(2,1)S(1)} %pack.5), channel_id=1, source_target_pairs={{0,384},{1,97},{2,386},{3,99},{4,388},{5,101},{6,390},{7,103},{8,3... | collective-permute-start | bytes 2359304 | tf_op jit(solution)/shard_map/ppermute | solution.py:40
  16.4 3.4 %collective-permute-done.got = bf16[4,8,96,128]{3,2,1,0:T(8,128)(2,1)S(1)} collective-permute-done((bf16[4,8,96,128]{3,2,1,0:T(8,128)(2,1)S(1)}, bf16[4,8,96,128]{3,2,1,0:T(8,128)(2,1)S(1)}, u32[]{:S(2)}, u32[]{:S(2)}) %collective-permute-start) | collective-permute-done | bytes 786464 | tf_op jit(solution)/shard_map/ppermute | solution.py:40
  19.8 1.6 %early.1 = f32[4,5,96,128]{3,2,1,0:T(8,128)S(1)} custom-call(f32[64]{0:T(128)S(1)} %copy-done.7, f32[64]{0:T(128)S(1)} %add_multiply_fusion.tau, bf16[4,96,2048]{2,1,0:T(8,128)(2,1)S(1)} %copy-done.3, s32[4,96,2048]{2,1,0:T(8,128)S(1)} %copy-done.1, bf16[4,8,96,128]{3,2,1,0:T(8,128)(2,1)S(1)} %collective-permute-done.got), custom_call_target="tpu_custom_call" | custom-call | flops 8388608 | bytes 3145728 | tf_op jit(solution)/shard_map/early/pallas_call | solution.py:151
  21.4 4.7 %collective-permute-done.1.got_b = bf16[4,8,96,128]{3,2,1,0:T(8,128)(2,1)S(1)} collective-permute-done((bf16[4,8,96,128]{3,2,1,0:T(8,128)(2,1)S(1)}, bf16[4,8,96,128]{3,2,1,0:T(8,128)(2,1)S(1)}, u32[]{:S(2)}, u32[]{:S(2)}) %collective-permute-start.1) | collective-permute-done | bytes 786464 | tf_op jit(solution)/shard_map/ppermute | solution.py:40
  26.1 2.3 %collective-permute-done.2.got_c = bf16[4,8,96,128]{3,2,1,0:T(8,128)(2,1)S(1)} collective-permute-done((bf16[4,8,96,128]{3,2,1,0:T(8,128)(2,1)S(1)}, bf16[4,8,96,128]{3,2,1,0:T(8,128)(2,1)S(1)}, u32[]{:S(2)}, u32[]{:S(2)}) %collective-permute-start.2) | collective-permute-done | bytes 786464 | tf_op jit(solution)/shard_map/ppermute | solution.py:40
  29.2 2.4 %collective-permute-start.3 = (f32[5,96,128]{2,1,0:T(8,128)S(1)}, f32[5,96,128]{2,1,0:T(8,128)S(1)}, u32[]{:S(2)}, u32[]{:S(2)}) collective-permute-start(f32[5,96,128]{2,1,0:T(8,128)S(1)} %late.5), channel_id=1, source_target_pairs={{0,64},{1,257},{2,66},{3,259},{4,68},{5,261},{6,70},{7,263},{8,72}... | collective-permute-start | bytes 737288 | tf_op jit(solution)/shard_map/ppermute | solution.py:40
  32.4 3.4 %collective-permute-start.4 = (f32[5,96,128]{2,1,0:T(8,128)S(1)}, f32[5,96,128]{2,1,0:T(8,128)S(1)}, u32[]{:S(2)}, u32[]{:S(2)}) collective-permute-start(f32[5,96,128]{2,1,0:T(8,128)S(1)} %late.6), channel_id=1, source_target_pairs={{0,32},{1,129},{2,34},{3,131},{4,36},{5,133},{6,38},{7,135},{8,40}... | collective-permute-start | bytes 737288 | tf_op jit(solution)/shard_map/ppermute | solution.py:40
  36.6 2.3 %collective-permute-start.5 = (f32[5,96,128]{2,1,0:T(8,128)S(1)}, f32[5,96,128]{2,1,0:T(8,128)S(1)}, u32[]{:S(2)}, u32[]{:S(2)}) collective-permute-start(f32[5,96,128]{2,1,0:T(8,128)S(1)} %late.7), channel_id=1, source_target_pairs={{0,96},{1,385},{2,98},{3,387},{4,100},{5,389},{6,102},{7,391},{8,1... | collective-permute-start | bytes 737288 | tf_op jit(solution)/shard_map/ppermute | solution.py:40
  39.7 0.9 %collective-permute-done.4.got_b = f32[5,96,128]{2,1,0:T(8,128)S(1)} collective-permute-done((f32[5,96,128]{2,1,0:T(8,128)S(1)}, f32[5,96,128]{2,1,0:T(8,128)S(1)}, u32[]{:S(2)}, u32[]{:S(2)}) %collective-permute-start.4) | collective-permute-done | bytes 245792 | tf_op jit(solution)/shard_map/ppermute | solution.py:40
  40.6 3.4 %collective-permute-done.5.got_c = f32[5,96,128]{2,1,0:T(8,128)S(1)} collective-permute-done((f32[5,96,128]{2,1,0:T(8,128)S(1)}, f32[5,96,128]{2,1,0:T(8,128)S(1)}, u32[]{:S(2)}, u32[]{:S(2)}) %collective-permute-start.5) | collective-permute-done | bytes 245792 | tf_op jit(solution)/shard_map/ppermute | solution.py:40
  44.6 4.9 %collective-permute-start.6 = (f32[16,128]{1,0:T(8,128)S(1)}, f32[16,128]{1,0:T(8,128)S(1)}, u32[]{:S(2)}, u32[]{:S(2)}) collective-permute-start(f32[16,128]{1,0:T(8,128)S(1)} %get-tuple-element.9), channel_id=1, source_target_pairs={{0,32},{32,64},{64,96},{96,128},{128,160},{160,192},{192,224},{224... | collective-permute-start | bytes 24584 | tf_op jit(solution)/shard_map/ppermute | solution.py:337
  49.5 1.9 %collective-permute-start.7 = (f32[16,128]{1,0:T(8,128)S(1)}, f32[16,128]{1,0:T(8,128)S(1)}, u32[]{:S(2)}, u32[]{:S(2)}) collective-permute-start(f32[16,128]{1,0:T(8,128)S(1)} %get-tuple-element.10), channel_id=1, source_target_pairs={{32,0},{64,32},{96,64},{128,96},{160,128},{192,160},{224,192},{256... | collective-permute-start | bytes 24584 | tf_op jit(solution)/shard_map/ppermute | solution.py:337
  51.5 4.6 %collective-permute-done.7.after = f32[16,128]{1,0:T(8,128)S(1)} collective-permute-done((f32[16,128]{1,0:T(8,128)S(1)}, f32[16,128]{1,0:T(8,128)S(1)}, u32[]{:S(2)}, u32[]{:S(2)}) %collective-permute-start.7) | collective-permute-done | bytes 8224 | tf_op jit(solution)/shard_map/ppermute | solution.py:337
  56.9 8.8 %collective-permute-start.8 = (f32[32,128]{1,0:T(8,128)S(1)}, f32[32,128]{1,0:T(8,128)S(1)}, u32[]{:S(2)}, u32[]{:S(2)}) collective-permute-start(f32[32,128]{1,0:T(8,128)S(1)} %get-tuple-element.12), channel_id=1, source_target_pairs={{0,1},{1,2},{2,3},{3,4},{4,5},{5,6},{6,7},{7,8},{8,9},{9,10},{10,1... | collective-permute-start | bytes 49160 | tf_op jit(solution)/shard_map/ppermute | solution.py:337
  65.7 1.9 %collective-permute-start.9 = (f32[32,128]{1,0:T(8,128)S(1)}, f32[32,128]{1,0:T(8,128)S(1)}, u32[]{:S(2)}, u32[]{:S(2)}) collective-permute-start(f32[32,128]{1,0:T(8,128)S(1)} %get-tuple-element.13), channel_id=1, source_target_pairs={{1,0},{2,1},{3,2},{4,3},{5,4},{6,5},{7,6},{8,7},{9,8},{10,9},{11,1... | collective-permute-start | bytes 49160 | tf_op jit(solution)/shard_map/ppermute | solution.py:337
  68.3 3.7 %collective-permute-done.9.below = f32[32,128]{1,0:T(8,128)S(1)} collective-permute-done((f32[32,128]{1,0:T(8,128)S(1)}, f32[32,128]{1,0:T(8,128)S(1)}, u32[]{:S(2)}, u32[]{:S(2)}) %collective-permute-start.9) | collective-permute-done | bytes 16416 | tf_op jit(solution)/shard_map/ppermute | solution.py:337
  72.8 1.2 %curve.1 = f32[3,96,128]{2,1,0:T(8,128)} custom-call(s32[1,1]{1,0:T(1,128)S(6)} %copy.7.window, f32[96,128]{1,0:T(8,128)S(1)} %copy-done.5, f32[96,128]{1,0:T(8,128)S(1)} %get-tuple-element.11.sides, f32[32,128]{1,0:T(8,128)S(1)} %collective-permute-done.8.above, f32[32,128]{1,0:T(8,128)S(1)} %collective-permute-done.9.below), custom_call_target="tpu_custom_call" | custom-call | tf_op jit(solution)/shard_map/curve/pallas_call | solution.py:326
  (26 shorter events, 6.1 us)
Async XLA Ops:
  0.6 1.9 %copy-start = (s32[4,96,2048]{2,1,0:T(8,128)S(1)}, s32[4,96,2048]{2,1,0:T(8,128)}, u32[]{:S(2)}) copy-start(s32[4,96,2048]{2,1,0:T(8,128)} %mask.7) | copy-start | bytes 9437188
  2.5 1.4 %copy-start.2 = (bf16[4,96,2048]{2,1,0:T(8,128)(2,1)S(1)}, bf16[4,96,2048]{2,1,0:T(8,128)(2,1)}, u32[]{:S(2)}) copy-start(bf16[4,96,2048]{2,1,0:T(8,128)(2,1)} %anomaly.7) | copy-start | bytes 4718596
  3.9 0.7 copy-start.6
  5.5 14.2 %collective-permute-start = (bf16[4,8,96,128]{3,2,1,0:T(8,128)(2,1)S(1)}, bf16[4,8,96,128]{3,2,1,0:T(8,128)(2,1)S(1)}, u32[]{:S(2)}, u32[]{:S(2)}) collective-permute-start(bf16[4,8,96,128]{3,2,1,0:T(8,128)(2,1)S(1)} %pack.3), channel_id=1, source_target_pairs={{0,256},{1,65},{2,258},{3,67},{4,260},{5,69},{6,262},{7,71},{8,264... | collective-permute-start | bytes 2359304 | tf_op jit(solution)/shard_map/ppermute | solution.py:40
  9.4 7.0 %copy-start.8 = (s32[64]{0:T(128)S(1)}, s32[64]{0:T(128)}, u32[]{:S(2)}) copy-start(s32[64]{0:T(128)} %param.8) | copy-start | bytes 772
  9.4 10.4 %copy-start.1 = (s32[4,96,2048]{2,1,0:T(8,128)S(1)}, s32[4,96,2048]{2,1,0:T(8,128)}, u32[]{:S(2)}) copy-start(s32[4,96,2048]{2,1,0:T(8,128)} %mask.7) | copy-start | bytes 9437188
  9.4 10.4 %copy-start.3 = (bf16[4,96,2048]{2,1,0:T(8,128)(2,1)S(1)}, bf16[4,96,2048]{2,1,0:T(8,128)(2,1)}, u32[]{:S(2)}) copy-start(bf16[4,96,2048]{2,1,0:T(8,128)(2,1)} %anomaly.7) | copy-start | bytes 4718596
  9.4 10.4 %copy-start.7 = (f32[64]{0:T(128)S(1)}, f32[64]{0:T(128)}, u32[]{:S(2)}) copy-start(f32[64]{0:T(128)} %quality.7) | copy-start | bytes 772
  9.4 16.7 %collective-permute-start.1 = (bf16[4,8,96,128]{3,2,1,0:T(8,128)(2,1)S(1)}, bf16[4,8,96,128]{3,2,1,0:T(8,128)(2,1)S(1)}, u32[]{:S(2)}, u32[]{:S(2)}) collective-permute-start(bf16[4,8,96,128]{3,2,1,0:T(8,128)(2,1)S(1)} %pack.4), channel_id=1, source_target_pairs={{0,128},{1,33},{2,130},{3,35},{4,132},{5,37},{6,134},{7,39},{8,136... | collective-permute-start | bytes 2359304 | tf_op jit(solution)/shard_map/ppermute | solution.py:40
  14.5 13.9 %collective-permute-start.2 = (bf16[4,8,96,128]{3,2,1,0:T(8,128)(2,1)S(1)}, bf16[4,8,96,128]{3,2,1,0:T(8,128)(2,1)S(1)}, u32[]{:S(2)}, u32[]{:S(2)}) collective-permute-start(bf16[4,8,96,128]{3,2,1,0:T(8,128)(2,1)S(1)} %pack.5), channel_id=1, source_target_pairs={{0,384},{1,97},{2,386},{3,99},{4,388},{5,101},{6,390},{7,103},{8,3... | collective-permute-start | bytes 2359304 | tf_op jit(solution)/shard_map/ppermute | solution.py:40
  29.2 10.5 %collective-permute-start.3 = (f32[5,96,128]{2,1,0:T(8,128)S(1)}, f32[5,96,128]{2,1,0:T(8,128)S(1)}, u32[]{:S(2)}, u32[]{:S(2)}) collective-permute-start(f32[5,96,128]{2,1,0:T(8,128)S(1)} %late.5), channel_id=1, source_target_pairs={{0,64},{1,257},{2,66},{3,259},{4,68},{5,261},{6,70},{7,263},{8,72}... | collective-permute-start | bytes 737288 | tf_op jit(solution)/shard_map/ppermute | solution.py:40
  32.4 8.2 %collective-permute-start.4 = (f32[5,96,128]{2,1,0:T(8,128)S(1)}, f32[5,96,128]{2,1,0:T(8,128)S(1)}, u32[]{:S(2)}, u32[]{:S(2)}) collective-permute-start(f32[5,96,128]{2,1,0:T(8,128)S(1)} %late.6), channel_id=1, source_target_pairs={{0,32},{1,129},{2,34},{3,131},{4,36},{5,133},{6,38},{7,135},{8,40}... | collective-permute-start | bytes 737288 | tf_op jit(solution)/shard_map/ppermute | solution.py:40
  36.6 7.3 %collective-permute-start.5 = (f32[5,96,128]{2,1,0:T(8,128)S(1)}, f32[5,96,128]{2,1,0:T(8,128)S(1)}, u32[]{:S(2)}, u32[]{:S(2)}) collective-permute-start(f32[5,96,128]{2,1,0:T(8,128)S(1)} %late.7), channel_id=1, source_target_pairs={{0,96},{1,385},{2,98},{3,387},{4,100},{5,389},{6,102},{7,391},{8,1... | collective-permute-start | bytes 737288 | tf_op jit(solution)/shard_map/ppermute | solution.py:40
  44.6 6.9 %collective-permute-start.6 = (f32[16,128]{1,0:T(8,128)S(1)}, f32[16,128]{1,0:T(8,128)S(1)}, u32[]{:S(2)}, u32[]{:S(2)}) collective-permute-start(f32[16,128]{1,0:T(8,128)S(1)} %get-tuple-element.9), channel_id=1, source_target_pairs={{0,32},{32,64},{64,96},{96,128},{128,160},{160,192},{192,224},{224... | collective-permute-start | bytes 24584 | tf_op jit(solution)/shard_map/ppermute | solution.py:337
  49.5 6.5 %collective-permute-start.7 = (f32[16,128]{1,0:T(8,128)S(1)}, f32[16,128]{1,0:T(8,128)S(1)}, u32[]{:S(2)}, u32[]{:S(2)}) collective-permute-start(f32[16,128]{1,0:T(8,128)S(1)} %get-tuple-element.10), channel_id=1, source_target_pairs={{32,0},{64,32},{96,64},{128,96},{160,128},{192,160},{224,192},{256... | collective-permute-start | bytes 24584 | tf_op jit(solution)/shard_map/ppermute | solution.py:337
  56.1 0.8 %copy-start.4 = (f32[96,128]{1,0:T(8,128)S(1)}, f32[96,128]{1,0:T(8,128)}, u32[]{:S(2)}) copy-start(f32[96,128]{1,0:T(8,128)} %get-tuple-element.6.rate) | copy-start | bytes 147460
  56.9 11.3 %collective-permute-start.8 = (f32[32,128]{1,0:T(8,128)S(1)}, f32[32,128]{1,0:T(8,128)S(1)}, u32[]{:S(2)}, u32[]{:S(2)}) collective-permute-start(f32[32,128]{1,0:T(8,128)S(1)} %get-tuple-element.12), channel_id=1, source_target_pairs={{0,1},{1,2},{2,3},{3,4},{4,5},{5,6},{6,7},{7,8},{8,9},{9,10},{10,1... | collective-permute-start | bytes 49160 | tf_op jit(solution)/shard_map/ppermute | solution.py:337
  65.7 6.3 %collective-permute-start.9 = (f32[32,128]{1,0:T(8,128)S(1)}, f32[32,128]{1,0:T(8,128)S(1)}, u32[]{:S(2)}, u32[]{:S(2)}) collective-permute-start(f32[32,128]{1,0:T(8,128)S(1)} %get-tuple-element.13), channel_id=1, source_target_pairs={{1,0},{2,1},{3,2},{4,3},{5,4},{6,5},{7,6},{8,7},{9,8},{10,9},{11,1... | collective-permute-start | bytes 49160 | tf_op jit(solution)/shard_map/ppermute | solution.py:337
  72.0 0.8 %copy-start.5 = (f32[96,128]{1,0:T(8,128)S(1)}, f32[96,128]{1,0:T(8,128)}, u32[]{:S(2)}) copy-start(f32[96,128]{1,0:T(8,128)} %get-tuple-element.6.rate) | copy-start | bytes 147460

commit v2 on v1

v2 whole, which is shorter than its diff:
```python
import functools

import jax
import jax.numpy as jnp
from jax import lax
from jax.experimental import pallas as pl
from jax.experimental.pallas import tpu as pltpu
from jax.sharding import PartitionSpec as P

MAXH = 16
SIDE = 4
OWN = 4
ROWS = 96
COLS = 128
TILES = 32
AXES = ("epoch", "tile")
STEPS = (2, 1, -1)
ANY = pl.BlockSpec(memory_space=pl.ANY)
SMEM = pl.BlockSpec(memory_space=pltpu.SMEM)
VMEM = pl.BlockSpec(memory_space=pltpu.VMEM)
LIMIT = pltpu.CompilerParams(vmem_limit_bytes=12 << 20)
FIRST_LIMIT = pltpu.CompilerParams(vmem_limit_bytes=62 << 20)
STRIP = 16
BLOCKS = SIDE * SIDE
BESIDE = 2 * MAXH
SLOTS = SIDE + 1
TALL = 6 * ROWS + ROWS // SIDE


def ring_pairs(step, first):
    pairs = []
    for x in range(SIDE):
        for y in range(SIDE):
            for tile in range(TILES):
                if (tile % 2 == 0) == first:
                    there = (x + step) % SIDE * SIDE + y
                else:
                    there = x * SIDE + (y + step) % SIDE
                pairs.append(((x * SIDE + y) * TILES + tile, there * TILES + tile))
    return pairs


def shift(values, step, first):
    return lax.ppermute(values, AXES, ring_pairs(step, first))


def place():
    spot = lax.axis_index("epoch")
    even = lax.axis_index("tile") % 2 == 0
    x, y = spot // SIDE, spot % SIDE
    return jnp.where(even, x, y), jnp.where(even, y, x), even


def block_of(even, first, second):
    return jnp.where(even, SIDE * first + second, SIDE * second + first)


def epoch_of(even, first, second):
    return block_of(even, first, second) * OWN


def columns(block):
    return pl.ds(pl.multiple_of(block * COLS, COLS), COLS)


def lane(shape):
    return lax.broadcasted_iota(jnp.int32, shape, 1)


def group_of(shape):
    return (lane(shape) + MAXH) % COLS // BESIDE


def pack_epoch(step, own, quality, anomaly, mask, out):
    first, second, even = place()
    there = (first + step + SIDE) % SIDE
    weight = quality[epoch_of(even, first, second) + own]
    shape = (ROWS, COLS)
    ahead = lane(shape) < COLS // 2
    group = group_of(shape)
    levels = jnp.zeros(shape, jnp.bfloat16)
    heavies = jnp.zeros(shape, jnp.bfloat16)
    for slot in range(SIDE):
        block = block_of(even, there, slot)
        cols = columns(block)
        before, after = columns(jnp.maximum(block - 1, 0)), columns(jnp.minimum(block + 1, BLOCKS - 1))
        out[slot, own] = anomaly[own, :, cols]
        out[slot, OWN + own] = (mask[own, :, cols].astype(jnp.float32) * weight).astype(jnp.bfloat16)
        level = jnp.where(ahead, anomaly[own, :, after], anomaly[own, :, before])
        valid = jnp.where(ahead, mask[own, :, after], mask[own, :, before]).astype(jnp.float32)
        weights = jnp.where(
            lane((1, COLS)) < COLS // 2,
            jnp.where(block < BLOCKS - 1, weight, 0.0),
            jnp.where(block > 0, weight, 0.0),
        )
        heavy = (valid * weights).astype(jnp.bfloat16)
        if slot:
            level = pltpu.roll(level, slot * BESIDE, 1)
            heavy = pltpu.roll(heavy, slot * BESIDE, 1)
        levels = jnp.where(group == slot, level, levels)
        heavies = jnp.where(group == slot, heavy, heavies)
    out[SIDE, own] = levels
    out[SIDE, OWN + own] = heavies


PACKED = jax.ShapeDtypeStruct((SLOTS, 2 * OWN, ROWS, COLS), jnp.bfloat16)


def read_pack_kernel(steps, quality, anomaly, mask, *refs):
    outs, (level, valid, packed, sems, done) = refs[: len(steps)], refs[len(steps) :]
    copies = []
    for own in range(OWN):
        copies.append(pltpu.make_async_copy(mask.at[own], valid.at[own], sems.at[own, 0]))
        copies.append(pltpu.make_async_copy(anomaly.at[own], level.at[own], sems.at[own, 1]))
    for copy in copies:
        copy.start()
    writes = []
    for own in range(OWN):
        copies[2 * own].wait()
        copies[2 * own + 1].wait()
        for index, (step, out) in enumerate(zip(steps, outs)):
            pack_epoch(step, own, quality, level, valid, packed.at[index])
            for kind, which in enumerate((own, OWN + own)):
                writes.append(
                    pltpu.make_async_copy(packed.at[index, :, which], out.at[:, which], done.at[index, own, kind])
                )
                writes[-1].start()
    for write in writes:
        write.wait()


def read_packs(steps, quality, anomaly, mask):
    width = COLS * BLOCKS
    return pl.pallas_call(
        functools.partial(read_pack_kernel, steps),
        out_shape=(PACKED,) * len(steps),
        in_specs=[SMEM, ANY, ANY],
        out_specs=(ANY,) * len(steps),
        scratch_shapes=[
            pltpu.VMEM((OWN, ROWS, width), jnp.bfloat16),
            pltpu.VMEM((OWN, ROWS, width), jnp.int32),
            pltpu.VMEM((len(steps),) + PACKED.shape, jnp.bfloat16),
            pltpu.SemaphoreType.DMA((OWN, 2)),
            pltpu.SemaphoreType.DMA((len(steps), OWN, 2)),
        ],
        compiler_params=FIRST_LIMIT,
        cost_estimate=pl.CostEstimate(flops=1 << 20, bytes_accessed=5 << 20, transcendentals=0),
        name="read_pack",
    )(quality, anomaly, mask)


def pack_kernel(steps, quality, anomaly, mask, *outs):
    for step, out in zip(steps, outs):
        for own in range(OWN):
            pack_epoch(step, own, quality, anomaly, mask, out)


def packs(steps, quality, anomaly, mask):
    return pl.pallas_call(
        functools.partial(pack_kernel, steps),
        out_shape=(PACKED,) * len(steps),
        in_specs=[SMEM, VMEM, VMEM],
        out_specs=(VMEM,) * len(steps),
        compiler_params=LIMIT,
        cost_estimate=pl.CostEstimate(flops=1 << 20, bytes_accessed=3 << 20, transcendentals=0),
        name="pack",
    )(quality, anomaly, mask)


def added(totals, heavy, height, moment):
    timed = heavy * moment
    loaded = heavy * height
    terms = (heavy, timed, timed * moment, loaded, loaded * moment)
    return terms if totals is None else tuple(map(jnp.add, totals, terms))


def moments_of(tau, moved):
    first, second, even = place()
    base = epoch_of(even, (first - moved + SIDE) % SIDE, second)
    return [tau[base + own] for own in range(OWN)]


def more(totals, packed, slot, at, moments):
    for own in range(OWN):
        heavy = packed[slot, OWN + own, at].astype(jnp.float32)
        totals = added(totals, heavy, packed[slot, own, at].astype(jnp.float32), moments[own])
    return totals


def over_rows(body):
    for index in range(ROWS // STRIP):
        body(pl.ds(index * STRIP, STRIP))


def early_kernel(tau, own, got, out):
    near, far = moments_of(tau, 0), moments_of(tau, STEPS[0])
    for slot in range(SLOTS):

        def body(at):
            totals = more(more(None, own, slot, at, near), got, slot, at, far)
            for which, total in enumerate(totals):
                out[slot, which, at] = total

        over_rows(body)


def early_sums(tau, own, got):
    return pl.pallas_call(
        early_kernel,
        out_shape=jax.ShapeDtypeStruct((SLOTS, 5, ROWS, COLS), jnp.float32),
        in_specs=[SMEM, VMEM, VMEM],
        out_specs=VMEM,
        compiler_params=LIMIT,
        cost_estimate=pl.CostEstimate(flops=1 << 23, bytes_accessed=3 << 20, transcendentals=0),
        name="early",
    )(tau, own, got)


def beside_at(which):
    return pl.ds(which * ROWS, ROWS)


def late_kernel(tau, early, got_b, got_c, out, beside):
    moments = [moments_of(tau, moved) for moved in STEPS[1:]]

    def total_of(slot, at):
        totals = tuple(early[slot, which, at] for which in range(5))
        for got, moment in zip((got_b, got_c), moments):
            totals = more(totals, got, slot, at, moment)
        return totals

    for slot in range(SLOTS):

        def body(at):
            for which, total in enumerate(total_of(slot, at)):
                if slot < SIDE:
                    out[slot, pl.ds(which * ROWS + at.start, STRIP)] = total
                else:
                    beside[which, at] = total

        over_rows(body)
    quarter = ROWS // SIDE
    group = group_of((ROWS, COLS))
    short = group_of((quarter, COLS))

    def turned(values, count):
        return pltpu.roll(values, count % SIDE * BESIDE, 1) if count % SIDE else values

    for slot in range(SIDE):
        full = jnp.zeros((ROWS, COLS), jnp.float32)
        part = jnp.zeros((quarter, COLS), jnp.float32)
        for which in range(SIDE):
            full = jnp.where(group == which, turned(beside[which], which - slot), full)
            piece = beside[4, pl.ds(which * quarter, quarter)]
            part = jnp.where(short == which, turned(piece, which - slot), part)
        out[slot, pl.ds(5 * ROWS, ROWS)] = full
        out[slot, pl.ds(6 * ROWS, quarter)] = part


def late_sums(tau, early, got_b, got_c):
    return pl.pallas_call(
        late_kernel,
        out_shape=jax.ShapeDtypeStruct((SIDE, TALL, COLS), jnp.float32),
        in_specs=[SMEM, VMEM, VMEM, VMEM],
        out_specs=VMEM,
        scratch_shapes=[pltpu.VMEM((5, ROWS, COLS), jnp.float32)],
        compiler_params=LIMIT,
        cost_estimate=pl.CostEstimate(flops=1 << 23, bytes_accessed=4 << 20, transcendentals=0),
        name="late",
    )(tau, early, got_b, got_c)


def second_rings():
    rings = []
    for tile in range(TILES):
        for fixed in range(SIDE):
            spots = [fixed * SIDE + i if tile % 2 == 0 else i * SIDE + fixed for i in range(SIDE)]
            rings.append([spot * TILES + tile for spot in spots])
    return rings


def slope_from(sums):
    lifted = sums[0] + 1.0
    return (lifted * sums[4] - sums[1] * sums[3]) / (lifted * (sums[2] + 1.0) - sums[1] * sums[1])


def rate_kernel(got, rate, again, sides, top, bottom):
    total = got[0] + got[1] + got[2] + got[3]
    value = slope_from([total[which * ROWS : (which + 1) * ROWS] for which in range(5)])
    full = total[5 * ROWS : 6 * ROWS]
    part = total[6 * ROWS :]

    def back(values, which):
        return pltpu.roll(values, COLS - which * BESIDE, 1) if which else values

    spread = [back(full, which) for which in range(4)]
    spread.append(jnp.concatenate([back(part, which) for which in range(SIDE)], axis=0))
    beside = jnp.where(group_of((ROWS, COLS)) == 0, slope_from(spread), 0.0)
    rate[...] = value
    again[...] = value
    sides[...] = beside
    top[...] = jnp.concatenate([value[:MAXH], beside[:MAXH]], axis=0)
    bottom[...] = jnp.concatenate([value[ROWS - MAXH :], beside[ROWS - MAXH :]], axis=0)


def fitted_rate(got):
    block = jax.ShapeDtypeStruct((ROWS, COLS), jnp.float32)
    edge = jax.ShapeDtypeStruct((2 * MAXH, COLS), jnp.float32)
    return pl.pallas_call(
        rate_kernel,
        out_shape=(block, block, block, edge, edge),
        in_specs=[VMEM],
        out_specs=(VMEM,) * 5,
        compiler_params=LIMIT,
        name="rate",
    )(got)


def three_parts(values):
    high = values.astype(jnp.bfloat16)
    rest = values - high.astype(jnp.float32)
    middle = rest.astype(jnp.bfloat16)
    low = (rest - middle.astype(jnp.float32)).astype(jnp.bfloat16)
    return high, middle, low


def taps(offset, half):
    inside = jnp.abs(offset) <= half
    flat = jnp.where(inside, 1.0, 0.0)
    slope = jnp.where(inside, offset, 0).astype(jnp.float32)
    return tuple(v.astype(jnp.bfloat16) for v in (flat, slope, slope * slope))


def product(left, right):
    return jnp.dot(left, right, preferred_element_type=jnp.float32)


def curve_kernel(window, rate, sides, above, below, out):
    half = window[0, 0]
    middle = (half * (half + 1)).astype(jnp.float32) / 3.0
    line = lax.broadcasted_iota(jnp.int32, (2 * COLS, COLS), 0)
    column = jnp.where(line < COLS + MAXH, line, jnp.where(line >= 2 * COLS - MAXH, line - 2 * COLS, 4 * COLS))
    across = jnp.concatenate(taps(column - lane((2 * COLS, COLS)), half), axis=1)
    tall = ROWS + 2 * MAXH
    spot = lane((ROWS, tall))
    row = jnp.where(spot < ROWS, spot, jnp.where(spot < ROWS + MAXH, spot - ROWS - MAXH, spot - MAXH))
    along = taps(row - lax.broadcasted_iota(jnp.int32, (ROWS, tall), 0), half)

    tile = lax.axis_index("tile")
    from_above = jnp.where(tile > 0, above[...], 0.0)
    from_below = jnp.where(tile < TILES - 1, below[...], 0.0)
    main = jnp.concatenate([rate[...], from_above[:MAXH], from_below[:MAXH]], axis=0)
    beside = jnp.concatenate([sides[...], from_above[MAXH:], from_below[MAXH:]], axis=0)
    parts = three_parts(jnp.concatenate([main, beside], axis=1))
    wide = product(parts[0], across) + product(parts[1], across) + product(parts[2], across)
    flat, slope, square = (wide[:, i * COLS : (i + 1) * COLS] for i in range(3))
    bowl = square - middle * flat

    def down(weights, values):
        a, b, c = (product(weights, part) for part in three_parts(values))
        return a + b + c

    bowl_x = down(along[0], bowl)
    bowl_y = down(along[2], flat) - middle * down(along[0], flat)
    twist = down(along[1], slope)

    taps_at = lax.broadcasted_iota(jnp.int32, (8, COLS), 1) - MAXH
    inside = jnp.abs(taps_at) <= half
    squares = (taps_at * taps_at).astype(jnp.float32)
    width = half.astype(jnp.float32)
    slope_norm = jnp.sum(jnp.where(inside, squares, 0.0), axis=1, keepdims=True)[0:1]
    bowls = squares - middle
    bowl_norm = jnp.sum(jnp.where(inside, bowls * bowls, 0.0), axis=1, keepdims=True)[0:1]
    bowl_scale = 2.0 * width * width / ((2.0 * width + 1.0) * bowl_norm)
    twist_scale = width * width / (slope_norm * slope_norm)
    out[0] = bowl_x * bowl_scale
    out[1] = bowl_y * bowl_scale
    out[2] = twist * twist_scale


def curvature_of(window, rate, sides, above, below):
    return pl.pallas_call(
        curve_kernel,
        out_shape=jax.ShapeDtypeStruct((3, ROWS, COLS), jnp.float32),
        in_specs=[SMEM, VMEM, VMEM, VMEM, VMEM],
        out_specs=VMEM,
        compiler_params=LIMIT,
        name="curve",
    )(window, rate, sides, above, below)


def per_device(anomaly, mask, epoch_weight, days, window):
    tau = (days.astype(jnp.float32) - 1826.5) / 365.25
    packed = read_packs(STEPS[:1], epoch_weight, anomaly, mask)
    packed += read_packs(STEPS[1:], epoch_weight, anomaly, mask)
    packed += packs((0,), epoch_weight, anomaly, mask)
    got = [shift(values, step, True) for step, values in zip(STEPS, packed)]
    early = early_sums(tau, packed[3], got[0])
    mine = late_sums(tau, early, got[1], got[2])
    rest = lax.all_to_all(mine, AXES, split_axis=0, concat_axis=0, tiled=True, axis_index_groups=second_rings())
    rate, again, sides, top, bottom = fitted_rate(rest)
    above = lax.ppermute(bottom, "tile", [(i, (i + 1) % TILES) for i in range(TILES)])
    below = lax.ppermute(top, "tile", [(i, (i - 1) % TILES) for i in range(TILES)])
    return rate, curvature_of(window, again, sides, above, below)


def solution(mesh):
    in_specs = (P("epoch", "tile", None), P("epoch", "tile", None), P(), P(), P("tile", "epoch"))
    out_specs = (P("tile", "epoch"), P(None, "tile", "epoch"))
    return jax.shard_map(
        per_device, mesh=mesh, in_specs=in_specs, out_specs=out_specs, check_vma=False
    )
```

time: 74.5 us -> 61.4 us (0.82)
  the two profiles are of different devices: /device:TPU:125 before, /device:TPU:24 now
where the time goes in v2:
time: 61.4 us; the launch traced here: 60.4 us
  blocking collectives  17.7 us (29%)
  starting transfers between devices  16.9 us (28%)
  Pallas kernels  14.7 us (24%)
  waiting for transfers between devices  7.76 us (13%)
  local copies, waits for them, and re-layouts  1.9 us (3%)
  between operations  1.39 us (2%)
    all_to_all x1, blocking collectives, per_device(): lax.all_to_all(mine, AXES, split_axis=0, concat_axis=0, tiled=True, axis_...  17.7 us
    ppermute x3, starting transfers between devices, shift(): return lax.ppermute(values, AXES, ring_pairs(step, first))  12.1 us
    pallas_call x2, Pallas kernels, read_packs(): pl.pallas_call(functools.partial(read_pack_kernel, steps), out_shape=(PAC...  8.32 us
    ppermute x3, waiting for transfers between devices, shift(): return lax.ppermute(values, AXES, ring_pairs(step, first))  6.97 us
    ppermute x1, starting transfers between devices, per_device(): lax.ppermute(top, 'tile', [(i, (i - 1) % TILES) for i in range(TILES)])  4.82 us
    unnamed x8, local copies, waits for them, and re-layouts  1.9 us
    pallas_call x1, Pallas kernels, early_sums(): pl.pallas_call(early_kernel, out_shape=jax.ShapeDtypeStruct((SLOTS, 5, RO...  1.87 us
    pallas_call x1, Pallas kernels, late_sums(): pl.pallas_call(late_kernel, out_shape=jax.ShapeDtypeStruct((SIDE, TALL, C...  1.41 us
  transfers between devices with their start and end apart: 5, of which 3 were waited for; matrix products, arithmetic and copies ran while one was open for 0% of the time, Pallas kernels for 12%

profile of v2, /device:TPU:24, one launch (start us, length us, event | category | flops | bytes accessed | tf_op | source)
XLA Modules:
  0.0 60.4 jit_solution(627147761567977307)
XLA Ops:
  0.6 4.0 %read_pack.2 = bf16[5,8,96,128]{3,2,1,0:T(8,128)(2,1)} custom-call(f32[64]{0:T(128)} %quality.5, bf16[4,96,2048]{2,1,0:T(8,128)(2,1)} %anomaly.5, s32[4,96,2048]{2,1,0:T(8,128)} %mask.5), custom_call_target="tpu_custom_call" | custom-call | flops 1048576 | bytes 5242880 | tf_op jit(solution)/shard_map/read_pack/pallas_call | solution.py:134
  4.6 0.0 copy-start.1
  4.7 0.0 copy-start.2
  4.7 5.1 %collective-permute-start = (bf16[5,8,96,128]{3,2,1,0:T(8,128)(2,1)}, bf16[5,8,96,128]{3,2,1,0:T(8,128)(2,1)}, u32[]{:S(2)}, u32[]{:S(2)}) collective-permute-start(bf16[5,8,96,128]{3,2,1,0:T(8,128)(2,1)} %read_pack.2), channel_id=1, source_target_pairs={{0,256},{1,65},{2,258},{3,67},{4,260},{5,69},{6,262},{7,71},{8,264... | collective-permute-start | bytes 2949128 | tf_op jit(solution)/shard_map/ppermute | solution.py:44
  9.7 4.3 %read_pack.3 = (bf16[5,8,96,128]{3,2,1,0:T(8,128)(2,1)}, bf16[5,8,96,128]{3,2,1,0:T(8,128)(2,1)}) custom-call(f32[64]{0:T(128)} %quality.5, bf16[4,96,2048]{2,1,0:T(8,128)(2,1)} %anomaly.5, s32[4,96,2048]{2,1,0:T(8,128)} %mask.5), custom_call_target="tpu_custom_call" | custom-call | flops 1048576 | bytes 5242880 | tf_op jit(solution)/shard_map/read_pack/pallas_call | solution.py:134
  14.1 2.5 %collective-permute-start.1 = (bf16[5,8,96,128]{3,2,1,0:T(8,128)(2,1)}, bf16[5,8,96,128]{3,2,1,0:T(8,128)(2,1)S(1)}, u32[]{:S(2)}, u32[]{:S(2)}) collective-permute-start(bf16[5,8,96,128]{3,2,1,0:T(8,128)(2,1)} %get-tuple-element.9), channel_id=1, source_target_pairs={{0,128},{1,33},{2,130},{3,35},{4,132},{5,37},{6,134},{7,39},{8,136... | collective-permute-start | bytes 2949128 | tf_op jit(solution)/shard_map/ppermute | solution.py:44
  16.6 4.6 %collective-permute-start.2 = (bf16[5,8,96,128]{3,2,1,0:T(8,128)(2,1)}, bf16[5,8,96,128]{3,2,1,0:T(8,128)(2,1)S(1)}, u32[]{:S(2)}, u32[]{:S(2)}) collective-permute-start(bf16[5,8,96,128]{3,2,1,0:T(8,128)(2,1)} %get-tuple-element.10), channel_id=1, source_target_pairs={{0,384},{1,97},{2,386},{3,99},{4,388},{5,101},{6,390},{7,103},{8,3... | collective-permute-start | bytes 2949128 | tf_op jit(solution)/shard_map/ppermute | solution.py:44
  21.1 0.0 copy-done.1
  21.1 0.0 copy-start
  21.2 1.9 %copy-done = s32[4,96,2048]{2,1,0:T(8,128)S(1)} copy-done((s32[4,96,2048]{2,1,0:T(8,128)S(1)}, s32[4,96,2048]{2,1,0:T(8,128)}, u32[]{:S(2)}) %copy-start) | copy-done | bytes 3145752
  23.0 1.2 %pack.1.own = bf16[5,8,96,128]{3,2,1,0:T(8,128)(2,1)S(1)} custom-call(f32[64]{0:T(128)S(1)} %copy-done.2, bf16[4,96,2048]{2,1,0:T(8,128)(2,1)S(1)} %copy-done.1, s32[4,96,2048]{2,1,0:T(8,128)S(1)} %copy-done), custom_call_target="tpu_custom_call" | custom-call | flops 1048576 | bytes 3145728 | tf_op jit(solution)/shard_map/pack/pallas_call | solution.py:159
  24.3 0.0 copy-done.3
  24.3 0.0 collective-permute-done.got
  24.3 1.9 %early.1 = f32[5,5,96,128]{3,2,1,0:T(8,128)S(1)} custom-call(f32[64]{0:T(128)S(1)} %add_multiply_fusion.tau, bf16[5,8,96,128]{3,2,1,0:T(8,128)(2,1)S(1)} %pack.1.own, bf16[5,8,96,128]{3,2,1,0:T(8,128)(2,1)} %collective-permute-done.got), custom_call_target="tpu_custom_call" | custom-call | flops 8388608 | bytes 3145728 | tf_op jit(solution)/shard_map/early/pallas_call | solution.py:208
  26.2 6.9 %collective-permute-done.1.got_b = bf16[5,8,96,128]{3,2,1,0:T(8,128)(2,1)S(1)} collective-permute-done((bf16[5,8,96,128]{3,2,1,0:T(8,128)(2,1)}, bf16[5,8,96,128]{3,2,1,0:T(8,128)(2,1)S(1)}, u32[]{:S(2)}, u32[]{:S(2)}) %collective-permute-start.1) | collective-permute-done | bytes 983072 | tf_op jit(solution)/shard_map/ppermute | solution.py:44
  33.0 0.1 collective-permute-done.2.got_c
  33.1 1.4 %late.1 = f32[4,600,128]{2,1,0:T(8,128)S(1)} custom-call(f32[64]{0:T(128)S(1)} %add_multiply_fusion.tau, f32[5,5,96,128]{3,2,1,0:T(8,128)S(1)} %early.1, bf16[5,8,96,128]{3,2,1,0:T(8,128)(2,1)S(1)} %collective-permute-done.1.got_b, bf16[5,8,96,128]{3,2,1,0:T(8,128)(2,1)S(1)} %collective-permute-done.2.got_c), custom_call_target="tpu_custom_call" | custom-call | flops 8388608 | bytes 4194304 | tf_op jit(solution)/shard_map/late/pallas_call | solution.py:261
  34.5 17.7 %all_to_all.5.got = f32[4,600,128]{2,1,0:T(8,128)S(1)} all-to-all(f32[4,600,128]{2,1,0:T(8,128)S(1)} %late.1), channel_id=1, replica_groups={{0,32,64,96},{128,160,192,224},{256,288,320,352},{384,416,448,480},{1,1..., dimensions={0} | all-to-all | bytes 2457600 | tf_op jit(solution)/shard_map/all_to_all | solution.py:400
  52.3 0.7 %rate.1 = (f32[96,128]{1,0:T(8,128)}, f32[96,128]{1,0:T(8,128)S(1)}, f32[96,128]{1,0:T(8,128)S(1)}, f32[32,128]{1,0:T(8,128)S(1)}, f32[32,128]{1,0:T(8,128)S(1)}) custom-call(f32[4,600,128]{2,1,0:T(8,128)S(1)} %all_to_all.5.got), custom_call_target="tpu_custom_call" | custom-call | tf_op jit(solution)/shard_map/rate/pallas_call | solution.py:309
  53.0 0.0 collective-permute-start.3
  53.0 4.8 %collective-permute-start.4 = (f32[32,128]{1,0:T(8,128)S(1)}, f32[32,128]{1,0:T(8,128)S(1)}, u32[]{:S(2)}, u32[]{:S(2)}) collective-permute-start(f32[32,128]{1,0:T(8,128)S(1)} %get-tuple-element.15), channel_id=1, source_target_pairs={{0,31},{1,0},{2,1},{3,2},{4,3},{5,4},{6,5},{7,6},{8,7},{9,8},{10,9... | collective-permute-start | bytes 49160 | tf_op jit(solution)/shard_map/ppermute | solution.py:403
  58.5 0.8 %collective-permute-done.3.above = f32[32,128]{1,0:T(8,128)S(1)} collective-permute-done((f32[32,128]{1,0:T(8,128)S(1)}, f32[32,128]{1,0:T(8,128)S(1)}, u32[]{:S(2)}, u32[]{:S(2)}) %collective-permute-start.3) | collective-permute-done | bytes 16416 | tf_op jit(solution)/shard_map/ppermute | solution.py:402
  59.2 0.0 collective-permute-done.4.below
  59.3 1.2 %curve.1 = f32[3,96,128]{2,1,0:T(8,128)} custom-call(s32[1,1]{1,0:T(1,128)S(6)} %copy.7.window, f32[96,128]{1,0:T(8,128)S(1)} %get-tuple-element.12.rate, f32[96,128]{1,0:T(8,128)S(1)} %get-tuple-element.13.sides, f32[32,128]{1,0:T(8,128)S(1)} %collective-permute-done.3.above, f32[32,128]{1,0:T(8,128)S(1)} %collective-permute-done.4.below), custom_call_target="tpu_custom_call" | custom-call | tf_op jit(solution)/shard_map/curve/pallas_call | solution.py:382
  (3 shorter events, 0.0 us)
Async XLA Ops:
  4.6 16.5 %copy-start.1 = (bf16[4,96,2048]{2,1,0:T(8,128)(2,1)S(1)}, bf16[4,96,2048]{2,1,0:T(8,128)(2,1)}, u32[]{:S(2)}) copy-start(bf16[4,96,2048]{2,1,0:T(8,128)(2,1)} %anomaly.5) | copy-start | bytes 4718596
  4.7 16.5 %copy-start.2 = (f32[64]{0:T(128)S(1)}, f32[64]{0:T(128)}, u32[]{:S(2)}) copy-start(f32[64]{0:T(128)} %quality.5) | copy-start | bytes 772
  4.7 19.6 %collective-permute-start = (bf16[5,8,96,128]{3,2,1,0:T(8,128)(2,1)}, bf16[5,8,96,128]{3,2,1,0:T(8,128)(2,1)}, u32[]{:S(2)}, u32[]{:S(2)}) collective-permute-start(bf16[5,8,96,128]{3,2,1,0:T(8,128)(2,1)} %read_pack.2), channel_id=1, source_target_pairs={{0,256},{1,65},{2,258},{3,67},{4,260},{5,69},{6,262},{7,71},{8,264... | collective-permute-start | bytes 2949128 | tf_op jit(solution)/shard_map/ppermute | solution.py:44
  14.1 19.0 %collective-permute-start.1 = (bf16[5,8,96,128]{3,2,1,0:T(8,128)(2,1)}, bf16[5,8,96,128]{3,2,1,0:T(8,128)(2,1)S(1)}, u32[]{:S(2)}, u32[]{:S(2)}) collective-permute-start(bf16[5,8,96,128]{3,2,1,0:T(8,128)(2,1)} %get-tuple-element.9), channel_id=1, source_target_pairs={{0,128},{1,33},{2,130},{3,35},{4,132},{5,37},{6,134},{7,39},{8,136... | collective-permute-start | bytes 2949128 | tf_op jit(solution)/shard_map/ppermute | solution.py:44
  16.6 16.6 %collective-permute-start.2 = (bf16[5,8,96,128]{3,2,1,0:T(8,128)(2,1)}, bf16[5,8,96,128]{3,2,1,0:T(8,128)(2,1)S(1)}, u32[]{:S(2)}, u32[]{:S(2)}) collective-permute-start(bf16[5,8,96,128]{3,2,1,0:T(8,128)(2,1)} %get-tuple-element.10), channel_id=1, source_target_pairs={{0,384},{1,97},{2,386},{3,99},{4,388},{5,101},{6,390},{7,103},{8,3... | collective-permute-start | bytes 2949128 | tf_op jit(solution)/shard_map/ppermute | solution.py:44
  21.1 1.9 %copy-start = (s32[4,96,2048]{2,1,0:T(8,128)S(1)}, s32[4,96,2048]{2,1,0:T(8,128)}, u32[]{:S(2)}) copy-start(s32[4,96,2048]{2,1,0:T(8,128)} %mask.5) | copy-start | bytes 9437188
  23.0 1.2 %copy-start.3 = (s32[64]{0:T(128)S(1)}, s32[64]{0:T(128)}, u32[]{:S(2)}) copy-start(s32[64]{0:T(128)} %param.8) | copy-start | bytes 772
  53.0 6.2 %collective-permute-start.3 = (f32[32,128]{1,0:T(8,128)S(1)}, f32[32,128]{1,0:T(8,128)S(1)}, u32[]{:S(2)}, u32[]{:S(2)}) collective-permute-start(f32[32,128]{1,0:T(8,128)S(1)} %get-tuple-element.14), channel_id=1, source_target_pairs={{0,1},{1,2},{2,3},{3,4},{4,5},{5,6},{6,7},{7,8},{8,9},{9,10},{10,1... | collective-permute-start | bytes 49160 | tf_op jit(solution)/shard_map/ppermute | solution.py:402
  53.0 6.3 %collective-permute-start.4 = (f32[32,128]{1,0:T(8,128)S(1)}, f32[32,128]{1,0:T(8,128)S(1)}, u32[]{:S(2)}, u32[]{:S(2)}) collective-permute-start(f32[32,128]{1,0:T(8,128)S(1)} %get-tuple-element.15), channel_id=1, source_target_pairs={{0,31},{1,0},{2,1},{3,2},{4,3},{5,4},{6,5},{7,6},{8,7},{9,8},{10,9... | collective-permute-start | bytes 49160 | tf_op jit(solution)/shard_map/ppermute | solution.py:403

commit v3 on v2

--- a/solution.py
+++ b/solution.py
@@ -106,20 +106,53 @@
 PACKED = jax.ShapeDtypeStruct((SLOTS, 2 * OWN, ROWS, COLS), jnp.bfloat16)
 
 
+def read_windows(steps, even, first):
+    if len(steps) > 1:
+        return (((0, BLOCKS),),) * 2
+    there = (first + steps[0] + SIDE) % SIDE
+    run = SIDE + 2
+    on_even = ((jnp.clip(SIDE * there - 1, 0, BLOCKS - run), run),)
+    on_odd = tuple((jnp.clip(SIDE * slot + there - 1, 0, BLOCKS - 3), 3) for slot in range(SIDE))
+    return on_even, on_odd
+
+
 def read_pack_kernel(steps, quality, anomaly, mask, *refs):
-    outs, (level, valid, packed, sems, done) = refs[: len(steps)], refs[len(steps) :]
-    copies = []
-    for own in range(OWN):
-        copies.append(pltpu.make_async_copy(mask.at[own], valid.at[own], sems.at[own, 0]))
-        copies.append(pltpu.make_async_copy(anomaly.at[own], level.at[own], sems.at[own, 1]))
-    for copy in copies:
-        copy.start()
+    outs, (level, valid, packed, own_quality, sems, done, ready) = refs[: len(steps)], refs[len(steps) :]
+    known = pltpu.make_async_copy(quality, own_quality, ready)
+    known.start()
+    first, second, even = place()
+    on_even, on_odd = read_windows(steps, even, first)
+
+    def reads(windows, own):
+        for index, (start, blocks) in enumerate(windows):
+            cols = pl.ds(pl.multiple_of(start * COLS, COLS), blocks * COLS)
+            yield pltpu.make_async_copy(mask.at[own, :, cols], valid.at[own, :, cols], sems.at[own, index, 0])
+            yield pltpu.make_async_copy(anomaly.at[own, :, cols], level.at[own, :, cols], sems.at[own, index, 1])
+
+    def on_parity(act):
+        if on_even is on_odd:
+            act(on_even)
+        else:
+            pl.when(even)(lambda: act(on_even))
+            pl.when(jnp.logical_not(even))(lambda: act(on_odd))
+
+    def start(windows):
+        for own in range(OWN):
+            for copy in reads(windows, own):
+                copy.start()
+
+    on_parity(start)
+    known.wait()
     writes = []
     for own in range(OWN):
-        copies[2 * own].wait()
-        copies[2 * own + 1].wait()
+
+        def wait(windows):
+            for copy in reads(windows, own):
+                copy.wait()
+
+        on_parity(wait)
         for index, (step, out) in enumerate(zip(steps, outs)):
-            pack_epoch(step, own, quality, level, valid, packed.at[index])
+            pack_epoch(step, own, own_quality, level, valid, packed.at[index])
             for kind, which in enumerate((own, OWN + own)):
                 writes.append(
                     pltpu.make_async_copy(packed.at[index, :, which], out.at[:, which], done.at[index, own, kind])
@@ -134,14 +167,16 @@
     return pl.pallas_call(
         functools.partial(read_pack_kernel, steps),
         out_shape=(PACKED,) * len(steps),
-        in_specs=[SMEM, ANY, ANY],
+        in_specs=[ANY, ANY, ANY],
         out_specs=(ANY,) * len(steps),
         scratch_shapes=[
             pltpu.VMEM((OWN, ROWS, width), jnp.bfloat16),
             pltpu.VMEM((OWN, ROWS, width), jnp.int32),
             pltpu.VMEM((len(steps),) + PACKED.shape, jnp.bfloat16),
-            pltpu.SemaphoreType.DMA((OWN, 2)),
+            pltpu.SMEM((BLOCKS * OWN,), jnp.float32),
+            pltpu.SemaphoreType.DMA((OWN, SIDE, 2)),
             pltpu.SemaphoreType.DMA((len(steps), OWN, 2)),
+            pltpu.SemaphoreType.DMA,
         ],
         compiler_params=FIRST_LIMIT,
         cost_estimate=pl.CostEstimate(flops=1 << 20, bytes_accessed=5 << 20, transcendentals=0),
@@ -192,8 +227,56 @@
         body(pl.ds(index * STRIP, STRIP))
 
 
-def early_kernel(tau, own, got, out):
+EDGES = 2 * MAXH
+TIMES = jax.ShapeDtypeStruct((2, OWN, STRIP, COLS), jnp.float32)
+PREPARED = (
+    jax.ShapeDtypeStruct((2 * COLS, 3 * COLS), jnp.bfloat16),
+    jax.ShapeDtypeStruct((3, ROWS, ROWS), jnp.bfloat16),
+    jax.ShapeDtypeStruct((3, EDGES, EDGES), jnp.bfloat16),
+    jax.ShapeDtypeStruct((3, 8, COLS), jnp.float32),
+)
+
+
+def taps(offset, half):
+    inside = jnp.abs(offset) <= half
+    flat = jnp.where(inside, 1.0, 0.0)
+    slope = jnp.where(inside, offset, 0).astype(jnp.float32)
+    return tuple(v.astype(jnp.bfloat16) for v in (flat, slope, slope * slope))
+
+
+def prepare(half, across, along, beyond, factors):
+    line = lax.broadcasted_iota(jnp.int32, (2 * COLS, COLS), 0)
+    column = jnp.where(line < COLS + MAXH, line, jnp.where(line >= 2 * COLS - MAXH, line - 2 * COLS, 4 * COLS))
+    across[...] = jnp.concatenate(taps(column - lane((2 * COLS, COLS)), half), axis=1)
+    shape = (ROWS, ROWS)
+    for which, tap in enumerate(taps(lane(shape) - lax.broadcasted_iota(jnp.int32, shape, 0), half)):
+        along[which] = tap
+    shape = (EDGES, EDGES)
+    spot = lane(shape)
+    mine = lax.broadcasted_iota(jnp.int32, shape, 0)
+    row = jnp.where(spot < MAXH, spot - MAXH, spot + ROWS - MAXH)
+    mine = jnp.where(mine < MAXH, mine, mine + ROWS - EDGES)
+    for which, tap in enumerate(taps(row - mine, half)):
+        beyond[which] = tap
+    middle = (half * (half + 1)).astype(jnp.float32) / 3.0
+    width = half.astype(jnp.float32)
+    taps_at = lane((8, COLS)) - MAXH
+    inside = jnp.abs(taps_at) <= half
+    squares = (taps_at * taps_at).astype(jnp.float32)
+    bowls = squares - middle
+    slope_norm = jnp.sum(jnp.where(inside, squares, 0.0), axis=1, keepdims=True)
+    bowl_norm = jnp.sum(jnp.where(inside, bowls * bowls, 0.0), axis=1, keepdims=True)
+    shape = (8, COLS)
+    factors[0] = jnp.full(shape, middle, jnp.float32)
+    factors[1] = jnp.broadcast_to(2.0 * width * width / ((2.0 * width + 1.0) * bowl_norm), shape)
+    factors[2] = jnp.broadcast_to(width * width / (slope_norm * slope_norm), shape)
+
+
+def early_kernel(tau, window, own, got, out, times, *prepared):
     near, far = moments_of(tau, 0), moments_of(tau, STEPS[0])
+    for index, moved in enumerate(STEPS[1:]):
+        for which, moment in enumerate(moments_of(tau, moved)):
+            times[index, which] = jnp.full((STRIP, COLS), moment, jnp.float32)
     for slot in range(SLOTS):
 
         def body(at):
@@ -202,26 +285,23 @@
                 out[slot, which, at] = total
 
         over_rows(body)
-
-
-def early_sums(tau, own, got):
+    prepare(window[0, 0], *prepared)
+
+
+def early_sums(tau, window, own, got):
     return pl.pallas_call(
         early_kernel,
-        out_shape=jax.ShapeDtypeStruct((SLOTS, 5, ROWS, COLS), jnp.float32),
-        in_specs=[SMEM, VMEM, VMEM],
-        out_specs=VMEM,
+        out_shape=(jax.ShapeDtypeStruct((SLOTS, 5, ROWS, COLS), jnp.float32), TIMES) + PREPARED,
+        in_specs=[SMEM, SMEM, VMEM, VMEM],
+        out_specs=(VMEM,) * 6,
         compiler_params=LIMIT,
         cost_estimate=pl.CostEstimate(flops=1 << 23, bytes_accessed=3 << 20, transcendentals=0),
         name="early",
-    )(tau, own, got)
-
-
-def beside_at(which):
-    return pl.ds(which * ROWS, ROWS)
-
-
-def late_kernel(tau, early, got_b, got_c, out, beside):
-    moments = [moments_of(tau, moved) for moved in STEPS[1:]]
+    )(tau, window, own, got)
+
+
+def late_kernel(times, early, got_b, got_c, out, beside):
+    moments = [[times[index, own] for own in range(OWN)] for index in range(2)]
 
     def total_of(slot, at):
         totals = tuple(early[slot, which, at] for which in range(5))
@@ -257,17 +337,17 @@
         out[slot, pl.ds(6 * ROWS, quarter)] = part
 
 
-def late_sums(tau, early, got_b, got_c):
+def late_sums(times, early, got_b, got_c):
     return pl.pallas_call(
         late_kernel,
         out_shape=jax.ShapeDtypeStruct((SIDE, TALL, COLS), jnp.float32),
-        in_specs=[SMEM, VMEM, VMEM, VMEM],
+        in_specs=[VMEM, VMEM, VMEM, VMEM],
         out_specs=VMEM,
         scratch_shapes=[pltpu.VMEM((5, ROWS, COLS), jnp.float32)],
         compiler_params=LIMIT,
         cost_estimate=pl.CostEstimate(flops=1 << 23, bytes_accessed=4 << 20, transcendentals=0),
         name="late",
-    )(tau, early, got_b, got_c)
+    )(times, early, got_b, got_c)
 
 
 def second_rings():
@@ -284,7 +364,7 @@
     return (lifted * sums[4] - sums[1] * sums[3]) / (lifted * (sums[2] + 1.0) - sums[1] * sums[1])
 
 
-def rate_kernel(got, rate, again, sides, top, bottom):
+def rate_kernel(got, rate, sides, top, bottom):
     total = got[0] + got[1] + got[2] + got[3]
     value = slope_from([total[which * ROWS : (which + 1) * ROWS] for which in range(5)])
     full = total[5 * ROWS : 6 * ROWS]
@@ -297,7 +377,6 @@
     spread.append(jnp.concatenate([back(part, which) for which in range(SIDE)], axis=0))
     beside = jnp.where(group_of((ROWS, COLS)) == 0, slope_from(spread), 0.0)
     rate[...] = value
-    again[...] = value
     sides[...] = beside
     top[...] = jnp.concatenate([value[:MAXH], beside[:MAXH]], axis=0)
     bottom[...] = jnp.concatenate([value[ROWS - MAXH :], beside[ROWS - MAXH :]], axis=0)
@@ -308,9 +387,9 @@
     edge = jax.ShapeDtypeStruct((2 * MAXH, COLS), jnp.float32)
     return pl.pallas_call(
         rate_kernel,
-        out_shape=(block, block, block, edge, edge),
+        out_shape=(block, block, edge, edge),
         in_specs=[VMEM],
-        out_specs=(VMEM,) * 5,
+        out_specs=(VMEM,) * 4,
         compiler_params=LIMIT,
         name="rate",
     )(got)
@@ -324,69 +403,90 @@
     return high, middle, low
 
 
-def taps(offset, half):
-    inside = jnp.abs(offset) <= half
-    flat = jnp.where(inside, 1.0, 0.0)
-    slope = jnp.where(inside, offset, 0).astype(jnp.float32)
-    return tuple(v.astype(jnp.bfloat16) for v in (flat, slope, slope * slope))
-
-
 def product(left, right):
     return jnp.dot(left, right, preferred_element_type=jnp.float32)
 
 
-def curve_kernel(window, rate, sides, above, below, out):
-    half = window[0, 0]
-    middle = (half * (half + 1)).astype(jnp.float32) / 3.0
-    line = lax.broadcasted_iota(jnp.int32, (2 * COLS, COLS), 0)
-    column = jnp.where(line < COLS + MAXH, line, jnp.where(line >= 2 * COLS - MAXH, line - 2 * COLS, 4 * COLS))
-    across = jnp.concatenate(taps(column - lane((2 * COLS, COLS)), half), axis=1)
-    tall = ROWS + 2 * MAXH
-    spot = lane((ROWS, tall))
-    row = jnp.where(spot < ROWS, spot, jnp.where(spot < ROWS + MAXH, spot - ROWS - MAXH, spot - MAXH))
-    along = taps(row - lax.broadcasted_iota(jnp.int32, (ROWS, tall), 0), half)
-
-    tile = lax.axis_index("tile")
-    from_above = jnp.where(tile > 0, above[...], 0.0)
-    from_below = jnp.where(tile < TILES - 1, below[...], 0.0)
-    main = jnp.concatenate([rate[...], from_above[:MAXH], from_below[:MAXH]], axis=0)
-    beside = jnp.concatenate([sides[...], from_above[MAXH:], from_below[MAXH:]], axis=0)
-    parts = three_parts(jnp.concatenate([main, beside], axis=1))
+def over_columns(values, across, middle):
+    parts = three_parts(values)
     wide = product(parts[0], across) + product(parts[1], across) + product(parts[2], across)
     flat, slope, square = (wide[:, i * COLS : (i + 1) * COLS] for i in range(3))
-    bowl = square - middle * flat
+    return flat, slope, square - middle * flat
+
+
+def over_lines(along, sums, middle):
+    flat, slope, bowl = sums
 
     def down(weights, values):
         a, b, c = (product(weights, part) for part in three_parts(values))
         return a + b + c
 
-    bowl_x = down(along[0], bowl)
-    bowl_y = down(along[2], flat) - middle * down(along[0], flat)
-    twist = down(along[1], slope)
-
-    taps_at = lax.broadcasted_iota(jnp.int32, (8, COLS), 1) - MAXH
-    inside = jnp.abs(taps_at) <= half
-    squares = (taps_at * taps_at).astype(jnp.float32)
-    width = half.astype(jnp.float32)
-    slope_norm = jnp.sum(jnp.where(inside, squares, 0.0), axis=1, keepdims=True)[0:1]
-    bowls = squares - middle
-    bowl_norm = jnp.sum(jnp.where(inside, bowls * bowls, 0.0), axis=1, keepdims=True)[0:1]
-    bowl_scale = 2.0 * width * width / ((2.0 * width + 1.0) * bowl_norm)
-    twist_scale = width * width / (slope_norm * slope_norm)
-    out[0] = bowl_x * bowl_scale
-    out[1] = bowl_y * bowl_scale
-    out[2] = twist * twist_scale
-
-
-def curvature_of(window, rate, sides, above, below):
-    return pl.pallas_call(
-        curve_kernel,
-        out_shape=jax.ShapeDtypeStruct((3, ROWS, COLS), jnp.float32),
-        in_specs=[SMEM, VMEM, VMEM, VMEM, VMEM],
-        out_specs=VMEM,
+    return down(along[0], bowl), down(along[2], flat) - middle * down(along[0], flat), down(along[1], slope)
+
+
+SCALE_OF = (1, 1, 2)
+INNER = ROWS - EDGES
+
+
+def within_kernel(fitted, sides, across, along, factors, inner, partial):
+    middle = factors[0, 0:1]
+    sums = over_columns(jnp.concatenate([fitted[...], sides[...]], axis=1), across[...], middle)
+    for which, value in enumerate(over_lines(along, sums, middle)):
+        inner[which] = value[MAXH : ROWS - MAXH] * factors[SCALE_OF[which], 0:1]
+        partial[which] = jnp.concatenate([value[:MAXH], value[ROWS - MAXH :]], axis=0)
+
+
+def within(fitted, sides, across, along, factors):
+    return pl.pallas_call(
+        within_kernel,
+        out_shape=(
+            jax.ShapeDtypeStruct((3, INNER, COLS), jnp.float32),
+            jax.ShapeDtypeStruct((3, EDGES, COLS), jnp.float32),
+        ),
+        in_specs=[VMEM] * 5,
+        out_specs=(VMEM, VMEM),
         compiler_params=LIMIT,
-        name="curve",
-    )(window, rate, sides, above, below)
+        cost_estimate=pl.CostEstimate(flops=1 << 27, bytes_accessed=1 << 20, transcendentals=0),
+        name="within",
+    )(fitted, sides, across, along, factors)
+
+
+def finish_kernel(across, beyond, factors, fitted, inner, partial, above, below, rate, out, edge, sems):
+    writes = [
+        pltpu.make_async_copy(fitted, rate, sems.at[0]),
+        pltpu.make_async_copy(inner, out.at[:, pl.ds(MAXH, INNER)], sems.at[1]),
+        pltpu.make_async_copy(edge.at[:, pl.ds(0, MAXH)], out.at[:, pl.ds(0, MAXH)], sems.at[2]),
+        pltpu.make_async_copy(edge.at[:, pl.ds(MAXH, MAXH)], out.at[:, pl.ds(ROWS - MAXH, MAXH)], sems.at[3]),
+    ]
+    for write in writes[:2]:
+        write.start()
+    middle = factors[0, 0:1]
+    tile = lax.axis_index("tile")
+    up = jnp.where(tile > 0, above[...], 0.0)
+    down = jnp.where(tile < TILES - 1, below[...], 0.0)
+    values = [jnp.concatenate([part[:MAXH], part[MAXH:]], axis=1) for part in (up, down)]
+    sums = over_columns(jnp.concatenate(values, axis=0), across[...], middle)
+    for which, value in enumerate(over_lines(beyond, sums, middle)):
+        edge[which] = (partial[which] + value) * factors[SCALE_OF[which], 0:1]
+    for write in writes[2:]:
+        write.start()
+    for write in writes:
+        write.wait()
+
+
+def finish(across, beyond, factors, fitted, inner, partial, above, below):
+    return pl.pallas_call(
+        finish_kernel,
+        out_shape=(
+            jax.ShapeDtypeStruct((ROWS, COLS), jnp.float32),
+            jax.ShapeDtypeStruct((3, ROWS, COLS), jnp.float32),
+        ),
+        in_specs=[VMEM] * 8,
+        out_specs=(ANY, ANY),
+        scratch_shapes=[pltpu.VMEM((3, EDGES, COLS), jnp.float32), pltpu.SemaphoreType.DMA((4,))],
+        compiler_params=LIMIT,
+        name="finish",
+    )(across, beyond, factors, fitted, inner, partial, above, below)
 
 
 def per_device(anomaly, mask, epoch_weight, days, window):
@@ -395,13 +495,14 @@
     packed += read_packs(STEPS[1:], epoch_weight, anomaly, mask)
     packed += packs((0,), epoch_weight, anomaly, mask)
     got = [shift(values, step, True) for step, values in zip(STEPS, packed)]
-    early = early_sums(tau, packed[3], got[0])
-    mine = late_sums(tau, early, got[1], got[2])
+    early, times, across, along, beyond, factors = early_sums(tau, window, packed[3], got[0])
+    mine = late_sums(times, early, got[1], got[2])
     rest = lax.all_to_all(mine, AXES, split_axis=0, concat_axis=0, tiled=True, axis_index_groups=second_rings())
-    rate, again, sides, top, bottom = fitted_rate(rest)
+    fitted, sides, top, bottom = fitted_rate(rest)
     above = lax.ppermute(bottom, "tile", [(i, (i + 1) % TILES) for i in range(TILES)])
     below = lax.ppermute(top, "tile", [(i, (i - 1) % TILES) for i in range(TILES)])
-    return rate, curvature_of(window, again, sides, above, below)
+    inner, partial = within(fitted, sides, across, along, factors)
+    return finish(across, beyond, factors, fitted, inner, partial, above, below)
 
 
 def solution(mesh):

time: 61.4 us -> 59.2 us (0.964)
  Pallas kernels: 14.7 us -> 12.5 us
    pallas_call x2, Pallas kernels: 8.32 us -> 6.71 us  [read_packs(): pl.pallas_call(functools.partial(read_pack_kernel, steps), out_shape=(PAC...]
    pallas_call x3 -> x4, Pallas kernels: 3.79 us -> 3.61 us  [the longest x1 1.93 us: early_sums(): pl.pallas_call(early_kernel, out_shape=(jax.ShapeDtypeStruct((SLOTS, 5, R...]
  transfers between devices with their start and end apart: 5 -> 5, of which waited for: 3 -> 3; matrix products, arithmetic and copies ran while one was open for 0% -> 0% of each run, Pallas kernels for 12% -> 13%
where the time goes in v3:
time: 59.2 us; the launch traced here: 58.7 us
  blocking collectives  17.7 us (30%)
  starting transfers between devices  17.5 us (30%)
  Pallas kernels  12.5 us (21%)
  waiting for transfers between devices  7.65 us (13%)
  local copies, waits for them, and re-layouts  1.9 us (3%)
  between operations  1.41 us (2%)
    all_to_all x1, blocking collectives, per_device(): lax.all_to_all(mine, AXES, split_axis=0, concat_axis=0, tiled=True, axis_...  17.7 us
    ppermute x3, starting transfers between devices, shift(): return lax.ppermute(values, AXES, ring_pairs(step, first))  12.1 us
    pallas_call x2, Pallas kernels, read_packs(): pl.pallas_call(functools.partial(read_pack_kernel, steps), out_shape=(PAC...  6.71 us
    ppermute x3, waiting for transfers between devices, shift(): return lax.ppermute(values, AXES, ring_pairs(step, first))  6.7 us
    ppermute x1, starting transfers between devices, per_device(): lax.ppermute(top, 'tile', [(i, (i - 1) % TILES) for i in range(TILES)])  5.39 us
    pallas_call x1, Pallas kernels, early_sums(): pl.pallas_call(early_kernel, out_shape=(jax.ShapeDtypeStruct((SLOTS, 5, R...  1.93 us
    unnamed x8, local copies, waits for them, and re-layouts  1.9 us
    pallas_call x1, Pallas kernels, packs(): pl.pallas_call(functools.partial(pack_kernel, steps), out_shape=(PACKED,)...  1.22 us
  transfers between devices with their start and end apart: 5, of which 3 were waited for; matrix products, arithmetic and copies ran while one was open for 0% of the time, Pallas kernels for 13%

profile of v3, /device:TPU:24, one launch (start us, length us, event | category | flops | bytes accessed | tf_op | source)
XLA Modules:
  0.0 58.7 jit_solution(2890524417076468563)
XLA Ops:
  0.6 2.8 %read_pack.2 = bf16[5,8,96,128]{3,2,1,0:T(8,128)(2,1)} custom-call(f32[64]{0:T(128)} %quality.5, bf16[4,96,2048]{2,1,0:T(8,128)(2,1)} %anomaly.5, s32[4,96,2048]{2,1,0:T(8,128)} %mask.5), custom_call_target="tpu_custom_call" | custom-call | flops 1048576 | bytes 5242880 | tf_op jit(solution)/shard_map/read_pack/pallas_call | solution.py:167
  3.5 0.0 copy-start.1
  3.5 0.0 copy-start.2
  3.5 5.1 %collective-permute-start = (bf16[5,8,96,128]{3,2,1,0:T(8,128)(2,1)}, bf16[5,8,96,128]{3,2,1,0:T(8,128)(2,1)}, u32[]{:S(2)}, u32[]{:S(2)}) collective-permute-start(bf16[5,8,96,128]{3,2,1,0:T(8,128)(2,1)} %read_pack.2), channel_id=1, source_target_pairs={{0,256},{1,65},{2,258},{3,67},{4,260},{5,69},{6,262},{7,71},{8,264... | collective-permute-start | bytes 2949128 | tf_op jit(solution)/shard_map/ppermute | solution.py:44
  8.6 3.9 %read_pack.3 = (bf16[5,8,96,128]{3,2,1,0:T(8,128)(2,1)}, bf16[5,8,96,128]{3,2,1,0:T(8,128)(2,1)}) custom-call(f32[64]{0:T(128)} %quality.5, bf16[4,96,2048]{2,1,0:T(8,128)(2,1)} %anomaly.5, s32[4,96,2048]{2,1,0:T(8,128)} %mask.5), custom_call_target="tpu_custom_call" | custom-call | flops 1048576 | bytes 5242880 | tf_op jit(solution)/shard_map/read_pack/pallas_call | solution.py:167
  12.4 2.5 %collective-permute-start.1 = (bf16[5,8,96,128]{3,2,1,0:T(8,128)(2,1)}, bf16[5,8,96,128]{3,2,1,0:T(8,128)(2,1)S(1)}, u32[]{:S(2)}, u32[]{:S(2)}) collective-permute-start(bf16[5,8,96,128]{3,2,1,0:T(8,128)(2,1)} %get-tuple-element.21), channel_id=1, source_target_pairs={{0,128},{1,33},{2,130},{3,35},{4,132},{5,37},{6,134},{7,39},{8,136... | collective-permute-start | bytes 2949128 | tf_op jit(solution)/shard_map/ppermute | solution.py:44
  15.0 4.6 %collective-permute-start.2 = (bf16[5,8,96,128]{3,2,1,0:T(8,128)(2,1)}, bf16[5,8,96,128]{3,2,1,0:T(8,128)(2,1)S(1)}, u32[]{:S(2)}, u32[]{:S(2)}) collective-permute-start(bf16[5,8,96,128]{3,2,1,0:T(8,128)(2,1)} %get-tuple-element.22), channel_id=1, source_target_pairs={{0,384},{1,97},{2,386},{3,99},{4,388},{5,101},{6,390},{7,103},{8,3... | collective-permute-start | bytes 2949128 | tf_op jit(solution)/shard_map/ppermute | solution.py:44
  20.2 0.0 copy-done.1
  20.2 0.0 copy-start
  20.2 1.9 %copy-done = s32[4,96,2048]{2,1,0:T(8,128)S(1)} copy-done((s32[4,96,2048]{2,1,0:T(8,128)S(1)}, s32[4,96,2048]{2,1,0:T(8,128)}, u32[]{:S(2)}) %copy-start) | copy-done | bytes 3145752
  22.1 1.2 %pack.1.own = bf16[5,8,96,128]{3,2,1,0:T(8,128)(2,1)S(1)} custom-call(f32[64]{0:T(128)S(1)} %copy-done.2, bf16[4,96,2048]{2,1,0:T(8,128)(2,1)S(1)} %copy-done.1, s32[4,96,2048]{2,1,0:T(8,128)S(1)} %copy-done), custom_call_target="tpu_custom_call" | custom-call | flops 1048576 | bytes 3145728 | tf_op jit(solution)/shard_map/pack/pallas_call | solution.py:194
  23.3 0.0 collective-permute-done.got
  23.3 1.9 %early.1 = (f32[5,5,96,128]{3,2,1,0:T(8,128)S(1)}, f32[2,4,16,128]{3,2,1,0:T(8,128)S(1)}, bf16[256,384]{1,0:T(8,128)(2,1)S(1)}, bf16[3,96,96]{2,1,0:T(8,128)(2,1...) custom-call(f32[64]{0:T(128)S(1)} %add_multiply_fusion.tau, s32[1,1]{1,0:T(1,128)S(6)} %copy.7.window, ...), custom_call_target="tpu_custom_call" | custom-call | flops 8388608 | bytes 3145728 | tf_op jit(solution)/shard_map/early/pallas_call | solution.py:292
  25.3 6.6 %collective-permute-done.1.got_b = bf16[5,8,96,128]{3,2,1,0:T(8,128)(2,1)S(1)} collective-permute-done((bf16[5,8,96,128]{3,2,1,0:T(8,128)(2,1)}, bf16[5,8,96,128]{3,2,1,0:T(8,128)(2,1)S(1)}, u32[]{:S(2)}, u32[]{:S(2)}) %collective-permute-start.1) | collective-permute-done | bytes 983072 | tf_op jit(solution)/shard_map/ppermute | solution.py:44
  31.9 0.1 collective-permute-done.2.got_c
  32.0 1.0 %late.1 = f32[4,600,128]{2,1,0:T(8,128)S(1)} custom-call(f32[2,4,16,128]{3,2,1,0:T(8,128)S(1)} %get-tuple-element.19.times, f32[5,5,96,128]{3,2,1,0:T(8,128)S(1)} %get-tuple-element.20.early, bf16[5,8,96,128]{3,2,1,0:T(8,128)(2,1)S(1)} %collective-permute-done.1.got_b, bf16[5,8,96,128]{3,2,1,0:T(8,128)(2,1)S(1)} %collective-permute-done.2.got_c), custom_call_target="tpu_custom_call" | custom-call | flops 8388608 | bytes 4194304 | tf_op jit(solution)/shard_map/late/pallas_call | solution.py:341
  32.9 17.7 %all_to_all.5.got = f32[4,600,128]{2,1,0:T(8,128)S(1)} all-to-all(f32[4,600,128]{2,1,0:T(8,128)S(1)} %late.1), channel_id=1, replica_groups={{0,32,64,96},{128,160,192,224},{256,288,320,352},{384,416,448,480},{1,1..., dimensions={0} | all-to-all | bytes 2457600 | tf_op jit(solution)/shard_map/all_to_all | solution.py:500
  50.7 0.1 rate.1
  50.8 0.0 collective-permute-start.3
  50.8 5.4 %collective-permute-start.4 = (f32[32,128]{1,0:T(8,128)S(1)}, f32[32,128]{1,0:T(8,128)S(1)}, u32[]{:S(2)}, u32[]{:S(2)}) collective-permute-start(f32[32,128]{1,0:T(8,128)S(1)} %get-tuple-element.29), channel_id=1, source_target_pairs={{0,31},{1,0},{2,1},{3,2},{4,3},{5,4},{6,5},{7,6},{8,7},{9,8},{10,9... | collective-permute-start | bytes 49160 | tf_op jit(solution)/shard_map/ppermute | solution.py:503
  56.2 0.5 within.1
  56.7 0.9 %collective-permute-done.3.above = f32[32,128]{1,0:T(8,128)S(1)} collective-permute-done((f32[32,128]{1,0:T(8,128)S(1)}, f32[32,128]{1,0:T(8,128)S(1)}, u32[]{:S(2)}, u32[]{:S(2)}) %collective-permute-start.3) | collective-permute-done | bytes 16416 | tf_op jit(solution)/shard_map/ppermute | solution.py:502
  57.6 0.0 collective-permute-done.4.below
  57.7 1.1 %finish.1 = (f32[96,128]{1,0:T(8,128)}, f32[3,96,128]{2,1,0:T(8,128)}) custom-call(bf16[256,384]{1,0:T(8,128)(2,1)S(1)} %get-tuple-element.16.across, bf16[3,32,32]{2,1,0:T(8,128)(2,1)S(1)} %get-tuple-element.17.beyond, f32[3,8,128]{2,1,0:T(8,128)S(1)} %get-tuple-element.18.factors, f32[96,128]{1,0:T(8,128)S(1)} %get-tuple-element.23.fitted, ...), custom_call_target="tpu_custom_call" | custom-call | tf_op jit(solution)/shard_map/finish/pallas_call | solution.py:478
  (4 shorter events, 0.0 us)
Async XLA Ops:
  3.5 16.7 %copy-start.1 = (bf16[4,96,2048]{2,1,0:T(8,128)(2,1)S(1)}, bf16[4,96,2048]{2,1,0:T(8,128)(2,1)}, u32[]{:S(2)}) copy-start(bf16[4,96,2048]{2,1,0:T(8,128)(2,1)} %anomaly.5) | copy-start | bytes 4718596
  3.5 16.7 %copy-start.2 = (f32[64]{0:T(128)S(1)}, f32[64]{0:T(128)}, u32[]{:S(2)}) copy-start(f32[64]{0:T(128)} %quality.5) | copy-start | bytes 772
  3.5 19.8 %collective-permute-start = (bf16[5,8,96,128]{3,2,1,0:T(8,128)(2,1)}, bf16[5,8,96,128]{3,2,1,0:T(8,128)(2,1)}, u32[]{:S(2)}, u32[]{:S(2)}) collective-permute-start(bf16[5,8,96,128]{3,2,1,0:T(8,128)(2,1)} %read_pack.2), channel_id=1, source_target_pairs={{0,256},{1,65},{2,258},{3,67},{4,260},{5,69},{6,262},{7,71},{8,264... | collective-permute-start | bytes 2949128 | tf_op jit(solution)/shard_map/ppermute | solution.py:44
  12.4 19.4 %collective-permute-start.1 = (bf16[5,8,96,128]{3,2,1,0:T(8,128)(2,1)}, bf16[5,8,96,128]{3,2,1,0:T(8,128)(2,1)S(1)}, u32[]{:S(2)}, u32[]{:S(2)}) collective-permute-start(bf16[5,8,96,128]{3,2,1,0:T(8,128)(2,1)} %get-tuple-element.21), channel_id=1, source_target_pairs={{0,128},{1,33},{2,130},{3,35},{4,132},{5,37},{6,134},{7,39},{8,136... | collective-permute-start | bytes 2949128 | tf_op jit(solution)/shard_map/ppermute | solution.py:44
  15.0 17.0 %collective-permute-start.2 = (bf16[5,8,96,128]{3,2,1,0:T(8,128)(2,1)}, bf16[5,8,96,128]{3,2,1,0:T(8,128)(2,1)S(1)}, u32[]{:S(2)}, u32[]{:S(2)}) collective-permute-start(bf16[5,8,96,128]{3,2,1,0:T(8,128)(2,1)} %get-tuple-element.22), channel_id=1, source_target_pairs={{0,384},{1,97},{2,386},{3,99},{4,388},{5,101},{6,390},{7,103},{8,3... | collective-permute-start | bytes 2949128 | tf_op jit(solution)/shard_map/ppermute | solution.py:44
  20.2 1.9 %copy-start = (s32[4,96,2048]{2,1,0:T(8,128)S(1)}, s32[4,96,2048]{2,1,0:T(8,128)}, u32[]{:S(2)}) copy-start(s32[4,96,2048]{2,1,0:T(8,128)} %mask.5) | copy-start | bytes 9437188
  22.1 1.2 %copy-start.3 = (s32[64]{0:T(128)S(1)}, s32[64]{0:T(128)}, u32[]{:S(2)}) copy-start(s32[64]{0:T(128)} %param.8) | copy-start | bytes 772
  50.8 6.8 %collective-permute-start.3 = (f32[32,128]{1,0:T(8,128)S(1)}, f32[32,128]{1,0:T(8,128)S(1)}, u32[]{:S(2)}, u32[]{:S(2)}) collective-permute-start(f32[32,128]{1,0:T(8,128)S(1)} %get-tuple-element.28), channel_id=1, source_target_pairs={{0,1},{1,2},{2,3},{3,4},{4,5},{5,6},{6,7},{7,8},{8,9},{9,10},{10,1... | collective-permute-start | bytes 49160 | tf_op jit(solution)/shard_map/ppermute | solution.py:502
  50.8 6.8 %collective-permute-start.4 = (f32[32,128]{1,0:T(8,128)S(1)}, f32[32,128]{1,0:T(8,128)S(1)}, u32[]{:S(2)}, u32[]{:S(2)}) collective-permute-start(f32[32,128]{1,0:T(8,128)S(1)} %get-tuple-element.29), channel_id=1, source_target_pairs={{0,31},{1,0},{2,1},{3,2},{4,3},{5,4},{6,5},{7,6},{8,7},{9,8},{10,9... | collective-permute-start | bytes 49160 | tf_op jit(solution)/shard_map/ppermute | solution.py:503

commit v4 on v3

--- a/solution.py
+++ b/solution.py
@@ -228,20 +228,27 @@
 
 
 EDGES = 2 * MAXH
+TAPS = 4
 TIMES = jax.ShapeDtypeStruct((2, OWN, STRIP, COLS), jnp.float32)
 PREPARED = (
-    jax.ShapeDtypeStruct((2 * COLS, 3 * COLS), jnp.bfloat16),
-    jax.ShapeDtypeStruct((3, ROWS, ROWS), jnp.bfloat16),
-    jax.ShapeDtypeStruct((3, EDGES, EDGES), jnp.bfloat16),
-    jax.ShapeDtypeStruct((3, 8, COLS), jnp.float32),
+    jax.ShapeDtypeStruct((2 * COLS, TAPS * COLS), jnp.bfloat16),
+    jax.ShapeDtypeStruct((TAPS, ROWS, ROWS), jnp.bfloat16),
+    jax.ShapeDtypeStruct((TAPS, EDGES, EDGES), jnp.bfloat16),
+    jax.ShapeDtypeStruct((2, 8, COLS), jnp.float32),
 )
+
+
+def bowl_taps(offset, half):
+    return (3 * offset * offset - half * (half + 1)).astype(jnp.float32)
 
 
 def taps(offset, half):
     inside = jnp.abs(offset) <= half
-    flat = jnp.where(inside, 1.0, 0.0)
-    slope = jnp.where(inside, offset, 0).astype(jnp.float32)
-    return tuple(v.astype(jnp.bfloat16) for v in (flat, slope, slope * slope))
+    flat = jnp.where(inside, 1.0, 0.0).astype(jnp.bfloat16)
+    slope = jnp.where(inside, offset, 0).astype(jnp.float32).astype(jnp.bfloat16)
+    bowl = jnp.where(inside, bowl_taps(offset, half), 0.0)
+    most = bowl.astype(jnp.bfloat16)
+    return flat, slope, most, (bowl - most.astype(jnp.float32)).astype(jnp.bfloat16)
 
 
 def prepare(half, across, along, beyond, factors):
@@ -258,18 +265,16 @@
     mine = jnp.where(mine < MAXH, mine, mine + ROWS - EDGES)
     for which, tap in enumerate(taps(row - mine, half)):
         beyond[which] = tap
-    middle = (half * (half + 1)).astype(jnp.float32) / 3.0
     width = half.astype(jnp.float32)
     taps_at = lane((8, COLS)) - MAXH
     inside = jnp.abs(taps_at) <= half
     squares = (taps_at * taps_at).astype(jnp.float32)
-    bowls = squares - middle
+    bowls = bowl_taps(taps_at, half)
     slope_norm = jnp.sum(jnp.where(inside, squares, 0.0), axis=1, keepdims=True)
     bowl_norm = jnp.sum(jnp.where(inside, bowls * bowls, 0.0), axis=1, keepdims=True)
     shape = (8, COLS)
-    factors[0] = jnp.full(shape, middle, jnp.float32)
-    factors[1] = jnp.broadcast_to(2.0 * width * width / ((2.0 * width + 1.0) * bowl_norm), shape)
-    factors[2] = jnp.broadcast_to(width * width / (slope_norm * slope_norm), shape)
+    factors[0] = jnp.broadcast_to(6.0 * width * width / ((2.0 * width + 1.0) * bowl_norm), shape)
+    factors[1] = jnp.broadcast_to(width * width / (slope_norm * slope_norm), shape)
 
 
 def early_kernel(tau, window, own, got, out, times, *prepared):
@@ -309,7 +314,7 @@
             totals = more(totals, got, slot, at, moment)
         return totals
 
-    for slot in range(SLOTS):
+    for slot in (SIDE,) + tuple(range(SIDE)):
 
         def body(at):
             for which, total in enumerate(total_of(slot, at)):
@@ -407,31 +412,30 @@
     return jnp.dot(left, right, preferred_element_type=jnp.float32)
 
 
-def over_columns(values, across, middle):
+def over_columns(values, across):
     parts = three_parts(values)
     wide = product(parts[0], across) + product(parts[1], across) + product(parts[2], across)
-    flat, slope, square = (wide[:, i * COLS : (i + 1) * COLS] for i in range(3))
-    return flat, slope, square - middle * flat
-
-
-def over_lines(along, sums, middle):
+    flat, slope, most, rest = (wide[:, i * COLS : (i + 1) * COLS] for i in range(TAPS))
+    return flat, slope, most + rest
+
+
+def over_lines(along, sums):
     flat, slope, bowl = sums
 
     def down(weights, values):
         a, b, c = (product(weights, part) for part in three_parts(values))
         return a + b + c
 
-    return down(along[0], bowl), down(along[2], flat) - middle * down(along[0], flat), down(along[1], slope)
-
-
-SCALE_OF = (1, 1, 2)
+    return down(along[0], bowl), down(along[2], flat) + down(along[3], flat), down(along[1], slope)
+
+
+SCALE_OF = (0, 0, 1)
 INNER = ROWS - EDGES
 
 
 def within_kernel(fitted, sides, across, along, factors, inner, partial):
-    middle = factors[0, 0:1]
-    sums = over_columns(jnp.concatenate([fitted[...], sides[...]], axis=1), across[...], middle)
-    for which, value in enumerate(over_lines(along, sums, middle)):
+    sums = over_columns(jnp.concatenate([fitted[...], sides[...]], axis=1), across[...])
+    for which, value in enumerate(over_lines(along, sums)):
         inner[which] = value[MAXH : ROWS - MAXH] * factors[SCALE_OF[which], 0:1]
         partial[which] = jnp.concatenate([value[:MAXH], value[ROWS - MAXH :]], axis=0)
 
@@ -460,13 +464,12 @@
     ]
     for write in writes[:2]:
         write.start()
-    middle = factors[0, 0:1]
     tile = lax.axis_index("tile")
     up = jnp.where(tile > 0, above[...], 0.0)
     down = jnp.where(tile < TILES - 1, below[...], 0.0)
     values = [jnp.concatenate([part[:MAXH], part[MAXH:]], axis=1) for part in (up, down)]
-    sums = over_columns(jnp.concatenate(values, axis=0), across[...], middle)
-    for which, value in enumerate(over_lines(beyond, sums, middle)):
+    sums = over_columns(jnp.concatenate(values, axis=0), across[...])
+    for which, value in enumerate(over_lines(beyond, sums)):
         edge[which] = (partial[which] + value) * factors[SCALE_OF[which], 0:1]
     for write in writes[2:]:
         write.start()

time: 59.2 us -> 59.1 us (level)
  no operation moved by 1% of the time
where the time goes in v4:
time: 59.1 us; the launch traced here: 58.7 us
  blocking collectives  17.7 us (30%)
  starting transfers between devices  17.5 us (30%)
  Pallas kernels  12.5 us (21%)
  waiting for transfers between devices  7.62 us (13%)
  local copies, waits for them, and re-layouts  1.9 us (3%)
  between operations  1.41 us (2%)
    all_to_all x1, blocking collectives, per_device(): lax.all_to_all(mine, AXES, split_axis=0, concat_axis=0, tiled=True, axis_...  17.7 us
    ppermute x3, starting transfers between devices, shift(): return lax.ppermute(values, AXES, ring_pairs(step, first))  12.1 us
    pallas_call x2, Pallas kernels, read_packs(): pl.pallas_call(functools.partial(read_pack_kernel, steps), out_shape=(PAC...  6.71 us
    ppermute x3, waiting for transfers between devices, shift(): return lax.ppermute(values, AXES, ring_pairs(step, first))  6.67 us
    ppermute x1, starting transfers between devices, per_device(): lax.ppermute(top, 'tile', [(i, (i - 1) % TILES) for i in range(TILES)])  5.39 us
    pallas_call x1, Pallas kernels, early_sums(): pl.pallas_call(early_kernel, out_shape=(jax.ShapeDtypeStruct((SLOTS, 5, R...  1.97 us
    unnamed x8, local copies, waits for them, and re-layouts  1.9 us
    pallas_call x1, Pallas kernels, packs(): pl.pallas_call(functools.partial(pack_kernel, steps), out_shape=(PACKED,)...  1.22 us
  transfers between devices with their start and end apart: 5, of which 3 were waited for; matrix products, arithmetic and copies ran while one was open for 0% of the time, Pallas kernels for 13%

profile of v4, /device:TPU:24, one launch (start us, length us, event | category | flops | bytes accessed | tf_op | source)
XLA Modules:
  0.0 58.7 jit_solution(7313814959189788770)
XLA Ops:
  0.6 2.8 %read_pack.2 = bf16[5,8,96,128]{3,2,1,0:T(8,128)(2,1)} custom-call(f32[64]{0:T(128)} %quality.5, bf16[4,96,2048]{2,1,0:T(8,128)(2,1)} %anomaly.5, s32[4,96,2048]{2,1,0:T(8,128)} %mask.5), custom_call_target="tpu_custom_call" | custom-call | flops 1048576 | bytes 5242880 | tf_op jit(solution)/shard_map/read_pack/pallas_call | solution.py:167
  3.5 0.0 copy-start.1
  3.5 0.0 copy-start.2
  3.5 5.1 %collective-permute-start = (bf16[5,8,96,128]{3,2,1,0:T(8,128)(2,1)}, bf16[5,8,96,128]{3,2,1,0:T(8,128)(2,1)}, u32[]{:S(2)}, u32[]{:S(2)}) collective-permute-start(bf16[5,8,96,128]{3,2,1,0:T(8,128)(2,1)} %read_pack.2), channel_id=1, source_target_pairs={{0,256},{1,65},{2,258},{3,67},{4,260},{5,69},{6,262},{7,71},{8,264... | collective-permute-start | bytes 2949128 | tf_op jit(solution)/shard_map/ppermute | solution.py:44
  8.6 3.9 %read_pack.3 = (bf16[5,8,96,128]{3,2,1,0:T(8,128)(2,1)}, bf16[5,8,96,128]{3,2,1,0:T(8,128)(2,1)}) custom-call(f32[64]{0:T(128)} %quality.5, bf16[4,96,2048]{2,1,0:T(8,128)(2,1)} %anomaly.5, s32[4,96,2048]{2,1,0:T(8,128)} %mask.5), custom_call_target="tpu_custom_call" | custom-call | flops 1048576 | bytes 5242880 | tf_op jit(solution)/shard_map/read_pack/pallas_call | solution.py:167
  12.4 2.5 %collective-permute-start.1 = (bf16[5,8,96,128]{3,2,1,0:T(8,128)(2,1)}, bf16[5,8,96,128]{3,2,1,0:T(8,128)(2,1)S(1)}, u32[]{:S(2)}, u32[]{:S(2)}) collective-permute-start(bf16[5,8,96,128]{3,2,1,0:T(8,128)(2,1)} %get-tuple-element.21), channel_id=1, source_target_pairs={{0,128},{1,33},{2,130},{3,35},{4,132},{5,37},{6,134},{7,39},{8,136... | collective-permute-start | bytes 2949128 | tf_op jit(solution)/shard_map/ppermute | solution.py:44
  15.0 4.6 %collective-permute-start.2 = (bf16[5,8,96,128]{3,2,1,0:T(8,128)(2,1)}, bf16[5,8,96,128]{3,2,1,0:T(8,128)(2,1)S(1)}, u32[]{:S(2)}, u32[]{:S(2)}) collective-permute-start(bf16[5,8,96,128]{3,2,1,0:T(8,128)(2,1)} %get-tuple-element.22), channel_id=1, source_target_pairs={{0,384},{1,97},{2,386},{3,99},{4,388},{5,101},{6,390},{7,103},{8,3... | collective-permute-start | bytes 2949128 | tf_op jit(solution)/shard_map/ppermute | solution.py:44
  20.2 0.0 copy-done.1
  20.2 0.0 copy-start
  20.2 1.9 %copy-done = s32[4,96,2048]{2,1,0:T(8,128)S(1)} copy-done((s32[4,96,2048]{2,1,0:T(8,128)S(1)}, s32[4,96,2048]{2,1,0:T(8,128)}, u32[]{:S(2)}) %copy-start) | copy-done | bytes 3145752
  22.1 1.2 %pack.1.own = bf16[5,8,96,128]{3,2,1,0:T(8,128)(2,1)S(1)} custom-call(f32[64]{0:T(128)S(1)} %copy-done.2, bf16[4,96,2048]{2,1,0:T(8,128)(2,1)S(1)} %copy-done.1, s32[4,96,2048]{2,1,0:T(8,128)S(1)} %copy-done), custom_call_target="tpu_custom_call" | custom-call | flops 1048576 | bytes 3145728 | tf_op jit(solution)/shard_map/pack/pallas_call | solution.py:194
  23.3 0.0 collective-permute-done.got
  23.3 2.0 %early.1 = (f32[5,5,96,128]{3,2,1,0:T(8,128)S(1)}, f32[2,4,16,128]{3,2,1,0:T(8,128)S(1)}, bf16[256,512]{1,0:T(8,128)(2,1)S(1)}, bf16[4,96,96]{2,1,0:T(8,128)(2,1...) custom-call(f32[64]{0:T(128)S(1)} %add_multiply_fusion.tau, s32[1,1]{1,0:T(1,128)S(6)} %copy.7.window, ...), custom_call_target="tpu_custom_call" | custom-call | flops 8388608 | bytes 3145728 | tf_op jit(solution)/shard_map/early/pallas_call | solution.py:297
  25.3 6.6 %collective-permute-done.1.got_b = bf16[5,8,96,128]{3,2,1,0:T(8,128)(2,1)S(1)} collective-permute-done((bf16[5,8,96,128]{3,2,1,0:T(8,128)(2,1)}, bf16[5,8,96,128]{3,2,1,0:T(8,128)(2,1)S(1)}, u32[]{:S(2)}, u32[]{:S(2)}) %collective-permute-start.1) | collective-permute-done | bytes 983072 | tf_op jit(solution)/shard_map/ppermute | solution.py:44
  31.9 0.1 collective-permute-done.2.got_c
  32.0 0.9 %late.1 = f32[4,600,128]{2,1,0:T(8,128)S(1)} custom-call(f32[2,4,16,128]{3,2,1,0:T(8,128)S(1)} %get-tuple-element.19.times, f32[5,5,96,128]{3,2,1,0:T(8,128)S(1)} %get-tuple-element.20.early, bf16[5,8,96,128]{3,2,1,0:T(8,128)(2,1)S(1)} %collective-permute-done.1.got_b, bf16[5,8,96,128]{3,2,1,0:T(8,128)(2,1)S(1)} %collective-permute-done.2.got_c), custom_call_target="tpu_custom_call" | custom-call | flops 8388608 | bytes 4194304 | tf_op jit(solution)/shard_map/late/pallas_call | solution.py:346
  32.9 17.7 %all_to_all.5.got = f32[4,600,128]{2,1,0:T(8,128)S(1)} all-to-all(f32[4,600,128]{2,1,0:T(8,128)S(1)} %late.1), channel_id=1, replica_groups={{0,32,64,96},{128,160,192,224},{256,288,320,352},{384,416,448,480},{1,1..., dimensions={0} | all-to-all | bytes 2457600 | tf_op jit(solution)/shard_map/all_to_all | solution.py:503
  50.6 0.1 rate.1
  50.7 0.0 collective-permute-start.3
  50.8 5.4 %collective-permute-start.4 = (f32[32,128]{1,0:T(8,128)S(1)}, f32[32,128]{1,0:T(8,128)S(1)}, u32[]{:S(2)}, u32[]{:S(2)}) collective-permute-start(f32[32,128]{1,0:T(8,128)S(1)} %get-tuple-element.29), channel_id=1, source_target_pairs={{0,31},{1,0},{2,1},{3,2},{4,3},{5,4},{6,5},{7,6},{8,7},{9,8},{10,9... | collective-permute-start | bytes 49160 | tf_op jit(solution)/shard_map/ppermute | solution.py:506
  56.2 0.5 within.1
  56.6 0.9 %collective-permute-done.3.above = f32[32,128]{1,0:T(8,128)S(1)} collective-permute-done((f32[32,128]{1,0:T(8,128)S(1)}, f32[32,128]{1,0:T(8,128)S(1)}, u32[]{:S(2)}, u32[]{:S(2)}) %collective-permute-start.3) | collective-permute-done | bytes 16416 | tf_op jit(solution)/shard_map/ppermute | solution.py:505
  57.6 0.0 collective-permute-done.4.below
  57.6 1.1 %finish.1 = (f32[96,128]{1,0:T(8,128)}, f32[3,96,128]{2,1,0:T(8,128)}) custom-call(bf16[256,512]{1,0:T(8,128)(2,1)S(1)} %get-tuple-element.16.across, bf16[4,32,32]{2,1,0:T(8,128)(2,1)S(1)} %get-tuple-element.17.beyond, f32[2,8,128]{2,1,0:T(8,128)S(1)} %get-tuple-element.18.factors, f32[96,128]{1,0:T(8,128)S(1)} %get-tuple-element.23.fitted, ...), custom_call_target="tpu_custom_call" | custom-call | tf_op jit(solution)/shard_map/finish/pallas_call | solution.py:481
  (4 shorter events, 0.0 us)
Async XLA Ops:
  3.5 16.7 %copy-start.1 = (bf16[4,96,2048]{2,1,0:T(8,128)(2,1)S(1)}, bf16[4,96,2048]{2,1,0:T(8,128)(2,1)}, u32[]{:S(2)}) copy-start(bf16[4,96,2048]{2,1,0:T(8,128)(2,1)} %anomaly.5) | copy-start | bytes 4718596
  3.5 16.7 %copy-start.2 = (f32[64]{0:T(128)S(1)}, f32[64]{0:T(128)}, u32[]{:S(2)}) copy-start(f32[64]{0:T(128)} %quality.5) | copy-start | bytes 772
  3.5 19.8 %collective-permute-start = (bf16[5,8,96,128]{3,2,1,0:T(8,128)(2,1)}, bf16[5,8,96,128]{3,2,1,0:T(8,128)(2,1)}, u32[]{:S(2)}, u32[]{:S(2)}) collective-permute-start(bf16[5,8,96,128]{3,2,1,0:T(8,128)(2,1)} %read_pack.2), channel_id=1, source_target_pairs={{0,256},{1,65},{2,258},{3,67},{4,260},{5,69},{6,262},{7,71},{8,264... | collective-permute-start | bytes 2949128 | tf_op jit(solution)/shard_map/ppermute | solution.py:44
  12.4 19.4 %collective-permute-start.1 = (bf16[5,8,96,128]{3,2,1,0:T(8,128)(2,1)}, bf16[5,8,96,128]{3,2,1,0:T(8,128)(2,1)S(1)}, u32[]{:S(2)}, u32[]{:S(2)}) collective-permute-start(bf16[5,8,96,128]{3,2,1,0:T(8,128)(2,1)} %get-tuple-element.21), channel_id=1, source_target_pairs={{0,128},{1,33},{2,130},{3,35},{4,132},{5,37},{6,134},{7,39},{8,136... | collective-permute-start | bytes 2949128 | tf_op jit(solution)/shard_map/ppermute | solution.py:44
  15.0 17.0 %collective-permute-start.2 = (bf16[5,8,96,128]{3,2,1,0:T(8,128)(2,1)}, bf16[5,8,96,128]{3,2,1,0:T(8,128)(2,1)S(1)}, u32[]{:S(2)}, u32[]{:S(2)}) collective-permute-start(bf16[5,8,96,128]{3,2,1,0:T(8,128)(2,1)} %get-tuple-element.22), channel_id=1, source_target_pairs={{0,384},{1,97},{2,386},{3,99},{4,388},{5,101},{6,390},{7,103},{8,3... | collective-permute-start | bytes 2949128 | tf_op jit(solution)/shard_map/ppermute | solution.py:44
  20.2 1.9 %copy-start = (s32[4,96,2048]{2,1,0:T(8,128)S(1)}, s32[4,96,2048]{2,1,0:T(8,128)}, u32[]{:S(2)}) copy-start(s32[4,96,2048]{2,1,0:T(8,128)} %mask.5) | copy-start | bytes 9437188
  22.1 1.2 %copy-start.3 = (s32[64]{0:T(128)S(1)}, s32[64]{0:T(128)}, u32[]{:S(2)}) copy-start(s32[64]{0:T(128)} %param.8) | copy-start | bytes 772
  50.7 6.8 %collective-permute-start.3 = (f32[32,128]{1,0:T(8,128)S(1)}, f32[32,128]{1,0:T(8,128)S(1)}, u32[]{:S(2)}, u32[]{:S(2)}) collective-permute-start(f32[32,128]{1,0:T(8,128)S(1)} %get-tuple-element.28), channel_id=1, source_target_pairs={{0,1},{1,2},{2,3},{3,4},{4,5},{5,6},{6,7},{7,8},{8,9},{9,10},{10,1... | collective-permute-start | bytes 49160 | tf_op jit(solution)/shard_map/ppermute | solution.py:505
  50.8 6.8 %collective-permute-start.4 = (f32[32,128]{1,0:T(8,128)S(1)}, f32[32,128]{1,0:T(8,128)S(1)}, u32[]{:S(2)}, u32[]{:S(2)}) collective-permute-start(f32[32,128]{1,0:T(8,128)S(1)} %get-tuple-element.29), channel_id=1, source_target_pairs={{0,31},{1,0},{2,1},{3,2},{4,3},{5,4},{6,5},{7,6},{8,7},{9,8},{10,9... | collective-permute-start | bytes 49160 | tf_op jit(solution)/shard_map/ppermute | solution.py:506

commit v5 on v4

--- a/solution.py
+++ b/solution.py
@@ -14,7 +14,7 @@
 COLS = 128
 TILES = 32
 AXES = ("epoch", "tile")
-STEPS = (2, 1, -1)
+STEPS = (2, -1, 1)
 ANY = pl.BlockSpec(memory_space=pl.ANY)
 SMEM = pl.BlockSpec(memory_space=pltpu.SMEM)
 VMEM = pl.BlockSpec(memory_space=pltpu.VMEM)
@@ -305,14 +305,36 @@
     )(tau, window, own, got)
 
 
-def late_kernel(times, early, got_b, got_c, out, beside):
-    moments = [[times[index, own] for own in range(OWN)] for index in range(2)]
+def middle_kernel(times, early, got, out):
+    for slot in range(SLOTS):
+
+        def body(at):
+            totals = tuple(early[slot, which, at] for which in range(5))
+            totals = more(totals, got, slot, at, [times[0, own] for own in range(OWN)])
+            for which, total in enumerate(totals):
+                out[slot, which, at] = total
+
+        over_rows(body)
+
+
+def middle_sums(times, early, got):
+    return pl.pallas_call(
+        middle_kernel,
+        out_shape=jax.ShapeDtypeStruct((SLOTS, 5, ROWS, COLS), jnp.float32),
+        in_specs=[VMEM, VMEM, VMEM],
+        out_specs=VMEM,
+        compiler_params=LIMIT,
+        cost_estimate=pl.CostEstimate(flops=1 << 22, bytes_accessed=4 << 20, transcendentals=0),
+        name="middle",
+    )(times, early, got)
+
+
+def late_kernel(times, early, got, out, beside):
+    moments = [times[1, own] for own in range(OWN)]
 
     def total_of(slot, at):
         totals = tuple(early[slot, which, at] for which in range(5))
-        for got, moment in zip((got_b, got_c), moments):
-            totals = more(totals, got, slot, at, moment)
-        return totals
+        return more(totals, got, slot, at, moments)
 
     for slot in (SIDE,) + tuple(range(SIDE)):
 
@@ -342,17 +364,17 @@
         out[slot, pl.ds(6 * ROWS, quarter)] = part
 
 
-def late_sums(times, early, got_b, got_c):
+def late_sums(times, early, got):
     return pl.pallas_call(
         late_kernel,
         out_shape=jax.ShapeDtypeStruct((SIDE, TALL, COLS), jnp.float32),
-        in_specs=[VMEM, VMEM, VMEM, VMEM],
+        in_specs=[VMEM, VMEM, VMEM],
         out_specs=VMEM,
         scratch_shapes=[pltpu.VMEM((5, ROWS, COLS), jnp.float32)],
         compiler_params=LIMIT,
         cost_estimate=pl.CostEstimate(flops=1 << 23, bytes_accessed=4 << 20, transcendentals=0),
         name="late",
-    )(times, early, got_b, got_c)
+    )(times, early, got)
 
 
 def second_rings():
@@ -459,10 +481,8 @@
     writes = [
         pltpu.make_async_copy(fitted, rate, sems.at[0]),
         pltpu.make_async_copy(inner, out.at[:, pl.ds(MAXH, INNER)], sems.at[1]),
-        pltpu.make_async_copy(edge.at[:, pl.ds(0, MAXH)], out.at[:, pl.ds(0, MAXH)], sems.at[2]),
-        pltpu.make_async_copy(edge.at[:, pl.ds(MAXH, MAXH)], out.at[:, pl.ds(ROWS - MAXH, MAXH)], sems.at[3]),
     ]
-    for write in writes[:2]:
+    for write in writes:
         write.start()
     tile = lax.axis_index("tile")
     up = jnp.where(tile > 0, above[...], 0.0)
@@ -471,8 +491,12 @@
     sums = over_columns(jnp.concatenate(values, axis=0), across[...])
     for which, value in enumerate(over_lines(beyond, sums)):
         edge[which] = (partial[which] + value) * factors[SCALE_OF[which], 0:1]
-    for write in writes[2:]:
-        write.start()
+        for end, row in enumerate((0, ROWS - MAXH)):
+            write = pltpu.make_async_copy(
+                edge.at[which, pl.ds(end * MAXH, MAXH)], out.at[which, pl.ds(row, MAXH)], sems.at[2 + 2 * which + end]
+            )
+            write.start()
+            writes.append(write)
     for write in writes:
         write.wait()
 
@@ -486,7 +510,7 @@
         ),
         in_specs=[VMEM] * 8,
         out_specs=(ANY, ANY),
-        scratch_shapes=[pltpu.VMEM((3, EDGES, COLS), jnp.float32), pltpu.SemaphoreType.DMA((4,))],
+        scratch_shapes=[pltpu.VMEM((3, EDGES, COLS), jnp.float32), pltpu.SemaphoreType.DMA((8,))],
         compiler_params=LIMIT,
         name="finish",
     )(across, beyond, factors, fitted, inner, partial, above, below)
@@ -499,7 +523,8 @@
     packed += packs((0,), epoch_weight, anomaly, mask)
     got = [shift(values, step, True) for step, values in zip(STEPS, packed)]
     early, times, across, along, beyond, factors = early_sums(tau, window, packed[3], got[0])
-    mine = late_sums(times, early, got[1], got[2])
+    middle = middle_sums(times, early, got[1])
+    mine = late_sums(times, middle, got[2])
     rest = lax.all_to_all(mine, AXES, split_axis=0, concat_axis=0, tiled=True, axis_index_groups=second_rings())
     fitted, sides, top, bottom = fitted_rate(rest)
     above = lax.ppermute(bottom, "tile", [(i, (i + 1) % TILES) for i in range(TILES)])

time: 59.1 us -> 59 us (level)
  waiting for transfers between devices: 7.62 us -> 9.44 us
  blocking collectives: 17.7 us -> 16.8 us
  starting transfers between devices: 17.5 us -> 16.7 us
    ppermute x3, waiting for transfers between devices: 6.67 us -> 8.47 us  [shift(): return lax.ppermute(values, AXES, ring_pairs(step, first))]
    ppermute x3, starting transfers between devices: 12.1 us -> 10.9 us  [shift(): return lax.ppermute(values, AXES, ring_pairs(step, first))]
    all_to_all x1, blocking collectives: 17.7 us -> 16.8 us  [per_device(): lax.all_to_all(mine, AXES, split_axis=0, concat_axis=0, tiled=True, axis_...]
where the time goes in v5:
time: 59 us; the launch traced here: 58.7 us
  blocking collectives  16.8 us (28%)
  starting transfers between devices  16.7 us (28%)
  Pallas kernels  12.5 us (21%)
  waiting for transfers between devices  9.44 us (16%)
  local copies, waits for them, and re-layouts  1.9 us (3%)
  between operations  1.41 us (2%)
    all_to_all x1, blocking collectives, per_device(): lax.all_to_all(mine, AXES, split_axis=0, concat_axis=0, tiled=True, axis_...  16.8 us
    ppermute x3, starting transfers between devices, shift(): return lax.ppermute(values, AXES, ring_pairs(step, first))  10.9 us
    ppermute x3, waiting for transfers between devices, shift(): return lax.ppermute(values, AXES, ring_pairs(step, first))  8.47 us
    pallas_call x2, Pallas kernels, read_packs(): pl.pallas_call(functools.partial(read_pack_kernel, steps), out_shape=(PAC...  6.71 us
    ppermute x1, starting transfers between devices, per_device(): lax.ppermute(top, 'tile', [(i, (i - 1) % TILES) for i in range(TILES)])  5.77 us
    pallas_call x1, Pallas kernels, early_sums(): pl.pallas_call(early_kernel, out_shape=(jax.ShapeDtypeStruct((SLOTS, 5, R...  1.97 us
    unnamed x8, local copies, waits for them, and re-layouts  1.9 us
    pallas_call x1, Pallas kernels, packs(): pl.pallas_call(functools.partial(pack_kernel, steps), out_shape=(PACKED,)...  1.22 us
  transfers between devices with their start and end apart: 5, of which 3 were waited for; matrix products, arithmetic and copies ran while one was open for 0% of the time, Pallas kernels for 13%

profile of v5, /device:TPU:24, one launch (start us, length us, event | category | flops | bytes accessed | tf_op | source)
XLA Modules:
  0.0 58.7 jit_solution(18320098972208931058)
XLA Ops:
  0.6 2.8 %read_pack.2 = bf16[5,8,96,128]{3,2,1,0:T(8,128)(2,1)} custom-call(f32[64]{0:T(128)} %quality.5, bf16[4,96,2048]{2,1,0:T(8,128)(2,1)} %anomaly.5, s32[4,96,2048]{2,1,0:T(8,128)} %mask.5), custom_call_target="tpu_custom_call" | custom-call | flops 1048576 | bytes 5242880 | tf_op jit(solution)/shard_map/read_pack/pallas_call | solution.py:167
  3.5 0.0 copy-start.1
  3.5 0.0 copy-start.2
  3.5 5.1 %collective-permute-start = (bf16[5,8,96,128]{3,2,1,0:T(8,128)(2,1)}, bf16[5,8,96,128]{3,2,1,0:T(8,128)(2,1)}, u32[]{:S(2)}, u32[]{:S(2)}) collective-permute-start(bf16[5,8,96,128]{3,2,1,0:T(8,128)(2,1)} %read_pack.2), channel_id=1, source_target_pairs={{0,256},{1,65},{2,258},{3,67},{4,260},{5,69},{6,262},{7,71},{8,264... | collective-permute-start | bytes 2949128 | tf_op jit(solution)/shard_map/ppermute | solution.py:44
  8.6 3.9 %read_pack.3 = (bf16[5,8,96,128]{3,2,1,0:T(8,128)(2,1)}, bf16[5,8,96,128]{3,2,1,0:T(8,128)(2,1)}) custom-call(f32[64]{0:T(128)} %quality.5, bf16[4,96,2048]{2,1,0:T(8,128)(2,1)} %anomaly.5, s32[4,96,2048]{2,1,0:T(8,128)} %mask.5), custom_call_target="tpu_custom_call" | custom-call | flops 1048576 | bytes 5242880 | tf_op jit(solution)/shard_map/read_pack/pallas_call | solution.py:167
  12.4 3.0 %collective-permute-start.1 = (bf16[5,8,96,128]{3,2,1,0:T(8,128)(2,1)}, bf16[5,8,96,128]{3,2,1,0:T(8,128)(2,1)S(1)}, u32[]{:S(2)}, u32[]{:S(2)}) collective-permute-start(bf16[5,8,96,128]{3,2,1,0:T(8,128)(2,1)} %get-tuple-element.21), channel_id=1, source_target_pairs={{0,384},{1,97},{2,386},{3,99},{4,388},{5,101},{6,390},{7,103},{8,3... | collective-permute-start | bytes 2949128 | tf_op jit(solution)/shard_map/ppermute | solution.py:44
  15.5 2.8 %collective-permute-start.2 = (bf16[5,8,96,128]{3,2,1,0:T(8,128)(2,1)}, bf16[5,8,96,128]{3,2,1,0:T(8,128)(2,1)S(1)}, u32[]{:S(2)}, u32[]{:S(2)}) collective-permute-start(bf16[5,8,96,128]{3,2,1,0:T(8,128)(2,1)} %get-tuple-element.22), channel_id=1, source_target_pairs={{0,128},{1,33},{2,130},{3,35},{4,132},{5,37},{6,134},{7,39},{8,136... | collective-permute-start | bytes 2949128 | tf_op jit(solution)/shard_map/ppermute | solution.py:44
  19.0 0.0 copy-start
  19.0 1.9 %copy-done = s32[4,96,2048]{2,1,0:T(8,128)S(1)} copy-done((s32[4,96,2048]{2,1,0:T(8,128)S(1)}, s32[4,96,2048]{2,1,0:T(8,128)}, u32[]{:S(2)}) %copy-start) | copy-done | bytes 3145752
  20.9 1.2 %pack.1.own = bf16[5,8,96,128]{3,2,1,0:T(8,128)(2,1)S(1)} custom-call(f32[64]{0:T(128)S(1)} %copy-done.2, bf16[4,96,2048]{2,1,0:T(8,128)(2,1)S(1)} %copy-done.1, s32[4,96,2048]{2,1,0:T(8,128)S(1)} %copy-done), custom_call_target="tpu_custom_call" | custom-call | flops 1048576 | bytes 3145728 | tf_op jit(solution)/shard_map/pack/pallas_call | solution.py:194
  22.1 0.0 collective-permute-done.got
  22.1 2.0 %early.1 = (f32[5,5,96,128]{3,2,1,0:T(8,128)S(1)}, f32[2,4,16,128]{3,2,1,0:T(8,128)S(1)}, bf16[256,512]{1,0:T(8,128)(2,1)S(1)}, bf16[4,96,96]{2,1,0:T(8,128)(2,1...) custom-call(f32[64]{0:T(128)S(1)} %add_multiply_fusion.tau, s32[1,1]{1,0:T(1,128)S(6)} %copy.7.window, ...), custom_call_target="tpu_custom_call" | custom-call | flops 8388608 | bytes 3145728 | tf_op jit(solution)/shard_map/early/pallas_call | solution.py:297
  24.1 7.9 %collective-permute-done.1.got = bf16[5,8,96,128]{3,2,1,0:T(8,128)(2,1)S(1)} collective-permute-done((bf16[5,8,96,128]{3,2,1,0:T(8,128)(2,1)}, bf16[5,8,96,128]{3,2,1,0:T(8,128)(2,1)S(1)}, u32[]{:S(2)}, u32[]{:S(2)}) %collective-permute-start.1) | collective-permute-done | bytes 983072 | tf_op jit(solution)/shard_map/ppermute | solution.py:44
  32.0 0.4 middle.1.early
  32.4 0.6 collective-permute-done.2.got
  32.9 0.6 late.1
  33.5 16.8 %all_to_all.5.got = f32[4,600,128]{2,1,0:T(8,128)S(1)} all-to-all(f32[4,600,128]{2,1,0:T(8,128)S(1)} %late.1), channel_id=1, replica_groups={{0,32,64,96},{128,160,192,224},{256,288,320,352},{384,416,448,480},{1,1..., dimensions={0} | all-to-all | bytes 2457600 | tf_op jit(solution)/shard_map/all_to_all | solution.py:528
  50.2 0.1 rate.1
  50.4 0.0 collective-permute-start.3
  50.4 5.8 %collective-permute-start.4 = (f32[32,128]{1,0:T(8,128)S(1)}, f32[32,128]{1,0:T(8,128)S(1)}, u32[]{:S(2)}, u32[]{:S(2)}) collective-permute-start(f32[32,128]{1,0:T(8,128)S(1)} %get-tuple-element.29), channel_id=1, source_target_pairs={{0,31},{1,0},{2,1},{3,2},{4,3},{5,4},{6,5},{7,6},{8,7},{9,8},{10,9... | collective-permute-start | bytes 49160 | tf_op jit(solution)/shard_map/ppermute | solution.py:531
  56.2 0.5 within.1
  56.6 0.9 %collective-permute-done.3.above = f32[32,128]{1,0:T(8,128)S(1)} collective-permute-done((f32[32,128]{1,0:T(8,128)S(1)}, f32[32,128]{1,0:T(8,128)S(1)}, u32[]{:S(2)}, u32[]{:S(2)}) %collective-permute-start.3) | collective-permute-done | bytes 16416 | tf_op jit(solution)/shard_map/ppermute | solution.py:530
  57.6 0.0 collective-permute-done.4.below
  57.6 1.1 %finish.1 = (f32[96,128]{1,0:T(8,128)}, f32[3,96,128]{2,1,0:T(8,128)}) custom-call(bf16[256,512]{1,0:T(8,128)(2,1)S(1)} %get-tuple-element.16.across, bf16[4,32,32]{2,1,0:T(8,128)(2,1)S(1)} %get-tuple-element.17.beyond, f32[2,8,128]{2,1,0:T(8,128)S(1)} %get-tuple-element.18.factors, f32[96,128]{1,0:T(8,128)S(1)} %get-tuple-element.23.fitted, ...), custom_call_target="tpu_custom_call" | custom-call | tf_op jit(solution)/shard_map/finish/pallas_call | solution.py:505
  (5 shorter events, 0.0 us)
Async XLA Ops:
  3.5 15.5 %copy-start.1 = (bf16[4,96,2048]{2,1,0:T(8,128)(2,1)S(1)}, bf16[4,96,2048]{2,1,0:T(8,128)(2,1)}, u32[]{:S(2)}) copy-start(bf16[4,96,2048]{2,1,0:T(8,128)(2,1)} %anomaly.5) | copy-start | bytes 4718596
  3.5 15.5 %copy-start.2 = (f32[64]{0:T(128)S(1)}, f32[64]{0:T(128)}, u32[]{:S(2)}) copy-start(f32[64]{0:T(128)} %quality.5) | copy-start | bytes 772
  3.5 18.6 %collective-permute-start = (bf16[5,8,96,128]{3,2,1,0:T(8,128)(2,1)}, bf16[5,8,96,128]{3,2,1,0:T(8,128)(2,1)}, u32[]{:S(2)}, u32[]{:S(2)}) collective-permute-start(bf16[5,8,96,128]{3,2,1,0:T(8,128)(2,1)} %read_pack.2), channel_id=1, source_target_pairs={{0,256},{1,65},{2,258},{3,67},{4,260},{5,69},{6,262},{7,71},{8,264... | collective-permute-start | bytes 2949128 | tf_op jit(solution)/shard_map/ppermute | solution.py:44
  12.4 19.6 %collective-permute-start.1 = (bf16[5,8,96,128]{3,2,1,0:T(8,128)(2,1)}, bf16[5,8,96,128]{3,2,1,0:T(8,128)(2,1)S(1)}, u32[]{:S(2)}, u32[]{:S(2)}) collective-permute-start(bf16[5,8,96,128]{3,2,1,0:T(8,128)(2,1)} %get-tuple-element.21), channel_id=1, source_target_pairs={{0,384},{1,97},{2,386},{3,99},{4,388},{5,101},{6,390},{7,103},{8,3... | collective-permute-start | bytes 2949128 | tf_op jit(solution)/shard_map/ppermute | solution.py:44
  15.5 17.4 %collective-permute-start.2 = (bf16[5,8,96,128]{3,2,1,0:T(8,128)(2,1)}, bf16[5,8,96,128]{3,2,1,0:T(8,128)(2,1)S(1)}, u32[]{:S(2)}, u32[]{:S(2)}) collective-permute-start(bf16[5,8,96,128]{3,2,1,0:T(8,128)(2,1)} %get-tuple-element.22), channel_id=1, source_target_pairs={{0,128},{1,33},{2,130},{3,35},{4,132},{5,37},{6,134},{7,39},{8,136... | collective-permute-start | bytes 2949128 | tf_op jit(solution)/shard_map/ppermute | solution.py:44
  19.0 1.9 %copy-start = (s32[4,96,2048]{2,1,0:T(8,128)S(1)}, s32[4,96,2048]{2,1,0:T(8,128)}, u32[]{:S(2)}) copy-start(s32[4,96,2048]{2,1,0:T(8,128)} %mask.5) | copy-start | bytes 9437188
  20.9 1.2 %copy-start.3 = (s32[64]{0:T(128)S(1)}, s32[64]{0:T(128)}, u32[]{:S(2)}) copy-start(s32[64]{0:T(128)} %param.8) | copy-start | bytes 772
  50.4 7.2 %collective-permute-start.3 = (f32[32,128]{1,0:T(8,128)S(1)}, f32[32,128]{1,0:T(8,128)S(1)}, u32[]{:S(2)}, u32[]{:S(2)}) collective-permute-start(f32[32,128]{1,0:T(8,128)S(1)} %get-tuple-element.28), channel_id=1, source_target_pairs={{0,1},{1,2},{2,3},{3,4},{4,5},{5,6},{6,7},{7,8},{8,9},{9,10},{10,1... | collective-permute-start | bytes 49160 | tf_op jit(solution)/shard_map/ppermute | solution.py:530
  50.4 7.2 %collective-permute-start.4 = (f32[32,128]{1,0:T(8,128)S(1)}, f32[32,128]{1,0:T(8,128)S(1)}, u32[]{:S(2)}, u32[]{:S(2)}) collective-permute-start(f32[32,128]{1,0:T(8,128)S(1)} %get-tuple-element.29), channel_id=1, source_target_pairs={{0,31},{1,0},{2,1},{3,2},{4,3},{5,4},{6,5},{7,6},{8,7},{9,8},{10,9... | collective-permute-start | bytes 49160 | tf_op jit(solution)/shard_map/ppermute | solution.py:531

commit v6 on v5

--- a/solution.py
+++ b/solution.py
@@ -527,8 +527,8 @@
     mine = late_sums(times, middle, got[2])
     rest = lax.all_to_all(mine, AXES, split_axis=0, concat_axis=0, tiled=True, axis_index_groups=second_rings())
     fitted, sides, top, bottom = fitted_rate(rest)
+    below = lax.ppermute(top, "tile", [(i, (i - 1) % TILES) for i in range(TILES)])
     above = lax.ppermute(bottom, "tile", [(i, (i + 1) % TILES) for i in range(TILES)])
-    below = lax.ppermute(top, "tile", [(i, (i - 1) % TILES) for i in range(TILES)])
     inner, partial = within(fitted, sides, across, along, factors)
     return finish(across, beyond, factors, fitted, inner, partial, above, below)
 

time: 59 us -> 59 us (level)
  no operation moved by 1% of the time
where the time goes in v6:
time: 59 us; the launch traced here: 58.7 us
  blocking collectives  16.8 us (28%)
  starting transfers between devices  16.7 us (28%)
  Pallas kernels  12.5 us (21%)
  waiting for transfers between devices  9.44 us (16%)
  local copies, waits for them, and re-layouts  1.9 us (3%)
  between operations  1.41 us (2%)
    all_to_all x1, blocking collectives, per_device(): lax.all_to_all(mine, AXES, split_axis=0, concat_axis=0, tiled=True, axis_...  16.8 us
    ppermute x3, starting transfers between devices, shift(): return lax.ppermute(values, AXES, ring_pairs(step, first))  10.9 us
    ppermute x3, waiting for transfers between devices, shift(): return lax.ppermute(values, AXES, ring_pairs(step, first))  8.47 us
    pallas_call x2, Pallas kernels, read_packs(): pl.pallas_call(functools.partial(read_pack_kernel, steps), out_shape=(PAC...  6.71 us
    ppermute x1, starting transfers between devices, per_device(): lax.ppermute(top, 'tile', [(i, (i - 1) % TILES) for i in range(TILES)])  5.77 us
    pallas_call x1, Pallas kernels, early_sums(): pl.pallas_call(early_kernel, out_shape=(jax.ShapeDtypeStruct((SLOTS, 5, R...  1.97 us
    unnamed x8, local copies, waits for them, and re-layouts  1.9 us
    pallas_call x1, Pallas kernels, packs(): pl.pallas_call(functools.partial(pack_kernel, steps), out_shape=(PACKED,)...  1.22 us
  transfers between devices with their start and end apart: 5, of which 3 were waited for; matrix products, arithmetic and copies ran while one was open for 0% of the time, Pallas kernels for 13%

profile of v6, /device:TPU:24, one launch (start us, length us, event | category | flops | bytes accessed | tf_op | source)
XLA Modules:
  0.0 58.7 jit_solution(18320098972208931058)
XLA Ops:
  0.6 2.8 %read_pack.2 = bf16[5,8,96,128]{3,2,1,0:T(8,128)(2,1)} custom-call(f32[64]{0:T(128)} %quality.5, bf16[4,96,2048]{2,1,0:T(8,128)(2,1)} %anomaly.5, s32[4,96,2048]{2,1,0:T(8,128)} %mask.5), custom_call_target="tpu_custom_call" | custom-call | flops 1048576 | bytes 5242880 | tf_op jit(solution)/shard_map/read_pack/pallas_call | solution.py:167
  3.5 0.0 copy-start.1
  3.5 0.0 copy-start.2
  3.5 5.1 %collective-permute-start = (bf16[5,8,96,128]{3,2,1,0:T(8,128)(2,1)}, bf16[5,8,96,128]{3,2,1,0:T(8,128)(2,1)}, u32[]{:S(2)}, u32[]{:S(2)}) collective-permute-start(bf16[5,8,96,128]{3,2,1,0:T(8,128)(2,1)} %read_pack.2), channel_id=1, source_target_pairs={{0,256},{1,65},{2,258},{3,67},{4,260},{5,69},{6,262},{7,71},{8,264... | collective-permute-start | bytes 2949128 | tf_op jit(solution)/shard_map/ppermute | solution.py:44
  8.6 3.9 %read_pack.3 = (bf16[5,8,96,128]{3,2,1,0:T(8,128)(2,1)}, bf16[5,8,96,128]{3,2,1,0:T(8,128)(2,1)}) custom-call(f32[64]{0:T(128)} %quality.5, bf16[4,96,2048]{2,1,0:T(8,128)(2,1)} %anomaly.5, s32[4,96,2048]{2,1,0:T(8,128)} %mask.5), custom_call_target="tpu_custom_call" | custom-call | flops 1048576 | bytes 5242880 | tf_op jit(solution)/shard_map/read_pack/pallas_call | solution.py:167
  12.4 3.0 %collective-permute-start.1 = (bf16[5,8,96,128]{3,2,1,0:T(8,128)(2,1)}, bf16[5,8,96,128]{3,2,1,0:T(8,128)(2,1)S(1)}, u32[]{:S(2)}, u32[]{:S(2)}) collective-permute-start(bf16[5,8,96,128]{3,2,1,0:T(8,128)(2,1)} %get-tuple-element.21), channel_id=1, source_target_pairs={{0,384},{1,97},{2,386},{3,99},{4,388},{5,101},{6,390},{7,103},{8,3... | collective-permute-start | bytes 2949128 | tf_op jit(solution)/shard_map/ppermute | solution.py:44
  15.5 2.8 %collective-permute-start.2 = (bf16[5,8,96,128]{3,2,1,0:T(8,128)(2,1)}, bf16[5,8,96,128]{3,2,1,0:T(8,128)(2,1)S(1)}, u32[]{:S(2)}, u32[]{:S(2)}) collective-permute-start(bf16[5,8,96,128]{3,2,1,0:T(8,128)(2,1)} %get-tuple-element.22), channel_id=1, source_target_pairs={{0,128},{1,33},{2,130},{3,35},{4,132},{5,37},{6,134},{7,39},{8,136... | collective-permute-start | bytes 2949128 | tf_op jit(solution)/shard_map/ppermute | solution.py:44
  19.0 0.0 copy-start
  19.0 1.9 %copy-done = s32[4,96,2048]{2,1,0:T(8,128)S(1)} copy-done((s32[4,96,2048]{2,1,0:T(8,128)S(1)}, s32[4,96,2048]{2,1,0:T(8,128)}, u32[]{:S(2)}) %copy-start) | copy-done | bytes 3145752
  20.9 1.2 %pack.1.own = bf16[5,8,96,128]{3,2,1,0:T(8,128)(2,1)S(1)} custom-call(f32[64]{0:T(128)S(1)} %copy-done.2, bf16[4,96,2048]{2,1,0:T(8,128)(2,1)S(1)} %copy-done.1, s32[4,96,2048]{2,1,0:T(8,128)S(1)} %copy-done), custom_call_target="tpu_custom_call" | custom-call | flops 1048576 | bytes 3145728 | tf_op jit(solution)/shard_map/pack/pallas_call | solution.py:194
  22.1 0.0 collective-permute-done.got
  22.1 2.0 %early.1 = (f32[5,5,96,128]{3,2,1,0:T(8,128)S(1)}, f32[2,4,16,128]{3,2,1,0:T(8,128)S(1)}, bf16[256,512]{1,0:T(8,128)(2,1)S(1)}, bf16[4,96,96]{2,1,0:T(8,128)(2,1...) custom-call(f32[64]{0:T(128)S(1)} %add_multiply_fusion.tau, s32[1,1]{1,0:T(1,128)S(6)} %copy.7.window, ...), custom_call_target="tpu_custom_call" | custom-call | flops 8388608 | bytes 3145728 | tf_op jit(solution)/shard_map/early/pallas_call | solution.py:297
  24.1 7.9 %collective-permute-done.1.got = bf16[5,8,96,128]{3,2,1,0:T(8,128)(2,1)S(1)} collective-permute-done((bf16[5,8,96,128]{3,2,1,0:T(8,128)(2,1)}, bf16[5,8,96,128]{3,2,1,0:T(8,128)(2,1)S(1)}, u32[]{:S(2)}, u32[]{:S(2)}) %collective-permute-start.1) | collective-permute-done | bytes 983072 | tf_op jit(solution)/shard_map/ppermute | solution.py:44
  32.0 0.4 middle.1.early
  32.4 0.6 collective-permute-done.2.got
  32.9 0.6 late.1
  33.5 16.8 %all_to_all.5.got = f32[4,600,128]{2,1,0:T(8,128)S(1)} all-to-all(f32[4,600,128]{2,1,0:T(8,128)S(1)} %late.1), channel_id=1, replica_groups={{0,32,64,96},{128,160,192,224},{256,288,320,352},{384,416,448,480},{1,1..., dimensions={0} | all-to-all | bytes 2457600 | tf_op jit(solution)/shard_map/all_to_all | solution.py:528
  50.2 0.1 rate.1
  50.4 0.0 collective-permute-start.3
  50.4 5.8 %collective-permute-start.4 = (f32[32,128]{1,0:T(8,128)S(1)}, f32[32,128]{1,0:T(8,128)S(1)}, u32[]{:S(2)}, u32[]{:S(2)}) collective-permute-start(f32[32,128]{1,0:T(8,128)S(1)} %get-tuple-element.29), channel_id=1, source_target_pairs={{0,31},{1,0},{2,1},{3,2},{4,3},{5,4},{6,5},{7,6},{8,7},{9,8},{10,9... | collective-permute-start | bytes 49160 | tf_op jit(solution)/shard_map/ppermute | solution.py:530
  56.2 0.5 within.1
  56.6 0.9 %collective-permute-done.3.above = f32[32,128]{1,0:T(8,128)S(1)} collective-permute-done((f32[32,128]{1,0:T(8,128)S(1)}, f32[32,128]{1,0:T(8,128)S(1)}, u32[]{:S(2)}, u32[]{:S(2)}) %collective-permute-start.3) | collective-permute-done | bytes 16416 | tf_op jit(solution)/shard_map/ppermute | solution.py:531
  57.6 0.0 collective-permute-done.4.below
  57.6 1.1 %finish.1 = (f32[96,128]{1,0:T(8,128)}, f32[3,96,128]{2,1,0:T(8,128)}) custom-call(bf16[256,512]{1,0:T(8,128)(2,1)S(1)} %get-tuple-element.16.across, bf16[4,32,32]{2,1,0:T(8,128)(2,1)S(1)} %get-tuple-element.17.beyond, f32[2,8,128]{2,1,0:T(8,128)S(1)} %get-tuple-element.18.factors, f32[96,128]{1,0:T(8,128)S(1)} %get-tuple-element.23.fitted, ...), custom_call_target="tpu_custom_call" | custom-call | tf_op jit(solution)/shard_map/finish/pallas_call | solution.py:505
  (5 shorter events, 0.0 us)
Async XLA Ops:
  3.5 15.5 %copy-start.1 = (bf16[4,96,2048]{2,1,0:T(8,128)(2,1)S(1)}, bf16[4,96,2048]{2,1,0:T(8,128)(2,1)}, u32[]{:S(2)}) copy-start(bf16[4,96,2048]{2,1,0:T(8,128)(2,1)} %anomaly.5) | copy-start | bytes 4718596
  3.5 15.5 %copy-start.2 = (f32[64]{0:T(128)S(1)}, f32[64]{0:T(128)}, u32[]{:S(2)}) copy-start(f32[64]{0:T(128)} %quality.5) | copy-start | bytes 772
  3.5 18.6 %collective-permute-start = (bf16[5,8,96,128]{3,2,1,0:T(8,128)(2,1)}, bf16[5,8,96,128]{3,2,1,0:T(8,128)(2,1)}, u32[]{:S(2)}, u32[]{:S(2)}) collective-permute-start(bf16[5,8,96,128]{3,2,1,0:T(8,128)(2,1)} %read_pack.2), channel_id=1, source_target_pairs={{0,256},{1,65},{2,258},{3,67},{4,260},{5,69},{6,262},{7,71},{8,264... | collective-permute-start | bytes 2949128 | tf_op jit(solution)/shard_map/ppermute | solution.py:44
  12.4 19.6 %collective-permute-start.1 = (bf16[5,8,96,128]{3,2,1,0:T(8,128)(2,1)}, bf16[5,8,96,128]{3,2,1,0:T(8,128)(2,1)S(1)}, u32[]{:S(2)}, u32[]{:S(2)}) collective-permute-start(bf16[5,8,96,128]{3,2,1,0:T(8,128)(2,1)} %get-tuple-element.21), channel_id=1, source_target_pairs={{0,384},{1,97},{2,386},{3,99},{4,388},{5,101},{6,390},{7,103},{8,3... | collective-permute-start | bytes 2949128 | tf_op jit(solution)/shard_map/ppermute | solution.py:44
  15.5 17.4 %collective-permute-start.2 = (bf16[5,8,96,128]{3,2,1,0:T(8,128)(2,1)}, bf16[5,8,96,128]{3,2,1,0:T(8,128)(2,1)S(1)}, u32[]{:S(2)}, u32[]{:S(2)}) collective-permute-start(bf16[5,8,96,128]{3,2,1,0:T(8,128)(2,1)} %get-tuple-element.22), channel_id=1, source_target_pairs={{0,128},{1,33},{2,130},{3,35},{4,132},{5,37},{6,134},{7,39},{8,136... | collective-permute-start | bytes 2949128 | tf_op jit(solution)/shard_map/ppermute | solution.py:44
  19.0 1.9 %copy-start = (s32[4,96,2048]{2,1,0:T(8,128)S(1)}, s32[4,96,2048]{2,1,0:T(8,128)}, u32[]{:S(2)}) copy-start(s32[4,96,2048]{2,1,0:T(8,128)} %mask.5) | copy-start | bytes 9437188
  20.9 1.2 %copy-start.3 = (s32[64]{0:T(128)S(1)}, s32[64]{0:T(128)}, u32[]{:S(2)}) copy-start(s32[64]{0:T(128)} %param.8) | copy-start | bytes 772
  50.4 7.2 %collective-permute-start.3 = (f32[32,128]{1,0:T(8,128)S(1)}, f32[32,128]{1,0:T(8,128)S(1)}, u32[]{:S(2)}, u32[]{:S(2)}) collective-permute-start(f32[32,128]{1,0:T(8,128)S(1)} %get-tuple-element.28), channel_id=1, source_target_pairs={{0,1},{1,2},{2,3},{3,4},{4,5},{5,6},{6,7},{7,8},{8,9},{9,10},{10,1... | collective-permute-start | bytes 49160 | tf_op jit(solution)/shard_map/ppermute | solution.py:531
  50.4 7.2 %collective-permute-start.4 = (f32[32,128]{1,0:T(8,128)S(1)}, f32[32,128]{1,0:T(8,128)S(1)}, u32[]{:S(2)}, u32[]{:S(2)}) collective-permute-start(f32[32,128]{1,0:T(8,128)S(1)} %get-tuple-element.29), channel_id=1, source_target_pairs={{0,31},{1,0},{2,1},{3,2},{4,3},{5,4},{6,5},{7,6},{8,7},{9,8},{10,9... | collective-permute-start | bytes 49160 | tf_op jit(solution)/shard_map/ppermute | solution.py:530
